TPU v7x, 512 devices: a whole 4x4x16 slice. The times are simulated.
512 devices in a mesh: client: 32 (over x, y, core), shard: 16 (over z).
Axes of the slice: x: 4, y: 4, z: 16, core: 2. Of those that a mesh axis runs over, the one named last changes fastest.
Arguments:
- updates: bfloat16 [384, 192, 14336], P('client', 'shard'), may hold values from -2000 to 2000
- momentum: float32 [192, 14336], P('shard', 'client'), may hold values from -6 to 6
- log_thresholds: float32 [12], replicated, may hold values from 0 to 20
- cohort_of: int32 [384], replicated, may hold values from 0 to 11, as said below
- seeds: int32 [8], replicated, may hold values from 0 to 1073741823
- round_index: int32 [1], replicated, may hold values from 8 to 99999
- coef_index: int32 [1], replicated, may hold values from 0 to 7
Outputs:
- momentum_next: float32 [192, 14336], P('shard', 'client')
- log_next: float32 [12], replicated
Inputs may be any that keep to these rules, and one draw needn't show every extreme that they name: `cohort_of`: each of the 12 cohorts is named by exactly 32 clients.
All inputs are finite; a program needn't handle non-finite values.
Results may differ from a plain program's by a relative error of at most 0.0003.
Values sent between devices are 32-bit elements; how exact they have to be, the bound alone decides.
No kernel may reach another device: no remote copies, remote signals or barrier semaphores. Data moves between devices by JAX's collectives and lax.ppermute only.
A program may use at most 64 MiB of HBM per device.

v0:
```python
import jax
import jax.numpy as jnp
from jax import lax
from jax.sharding import PartitionSpec as P


def mix(x):
    x = x ^ lax.shift_right_logical(x, jnp.int32(16))
    x = x * jnp.int32(2146121005)
    x = x ^ lax.shift_right_logical(x, jnp.int32(15))
    x = x * jnp.int32(-2073450869)
    x = x ^ lax.shift_right_logical(x, jnp.int32(16))
    return x


def band_noise(index, seeds, round_index, coef_index):
    lags = jnp.arange(seeds.shape[0], dtype=jnp.int32)
    keys = mix(seeds ^ (round_index[0] - lags) * jnp.int32(1640531527))
    hashed = mix(index[None] * jnp.int32(1013904223) + keys[:, None, None])
    uniform = (lax.shift_right_logical(hashed, jnp.int32(8)).astype(jnp.float32) + 0.5) * (
        1.0 / 16777216.0
    )
    normal_like = 3.4641016151377544 * (uniform - 0.5)
    rate = 0.4 + 0.07 * coef_index[0].astype(jnp.float32)
    lagf = lags.astype(jnp.float32)
    ratio = jnp.where(lags == 0, 1.0, rate * (2.0 * lagf - 1.0) / (2.0 * jnp.maximum(lagf, 1.0)))
    coefs = jnp.cumprod(ratio)
    return jnp.sum(coefs[:, None, None] * normal_like, axis=0)


def per_device(updates, momentum, log_thresholds, cohort_of, seeds, round_index, coef_index):
    local_clients = updates.shape[0]
    row_count = updates.shape[1]
    width = updates.shape[2]
    owned_cols = momentum.shape[1]
    cohort_count = log_thresholds.shape[0]
    total_clients = cohort_of.shape[0]
    client_pos = lax.axis_index("client")
    shard_pos = lax.axis_index("shard")
    limits = jnp.exp(log_thresholds)
    squares = jnp.sum(jnp.square(updates.astype(jnp.float32)), axis=(1, 2))
    own_cohort = lax.dynamic_slice_in_dim(cohort_of, client_pos * local_clients, local_clients)
    cohort_ids = jnp.arange(cohort_count, dtype=jnp.int32)
    own_member = (own_cohort[:, None] == cohort_ids[None, :]).astype(jnp.float32)
    own_limit = jnp.sum(own_member * limits[None, :], axis=1)
    norms = jnp.sqrt(lax.psum(squares, "shard"))
    own_bit = (norms <= own_limit).astype(jnp.float32)
    counts = lax.psum(jnp.sum(own_member * own_bit[:, None], axis=0), "client")
    factor = own_limit / jnp.maximum(norms, own_limit)
    local_sum = jnp.sum(factor[:, None, None] * updates.astype(jnp.float32), axis=0)
    owned = lax.psum_scatter(local_sum, "client", scatter_dimension=1, tiled=True)
    row_ids = shard_pos * row_count + jnp.arange(row_count, dtype=jnp.int32)
    col_ids = client_pos * owned_cols + jnp.arange(owned_cols, dtype=jnp.int32)
    index = row_ids[:, None] * jnp.int32(width) + col_ids[None, :]
    noise = band_noise(index, seeds, round_index, coef_index)
    aggregate = (owned + 0.05 * jnp.max(limits) * noise) / total_clients
    momentum_next = 0.9 * momentum + aggregate
    log_next = log_thresholds - 0.2 * (counts / (total_clients // cohort_count) - 0.5)
    return (momentum_next, log_next)


def solution(mesh):
    placed = (P("client", "shard", None), P("shard", "client"), P(), P(), P(), P(), P())
    return jax.shard_map(
        per_device,
        mesh=mesh,
        in_specs=placed,
        out_specs=(P("shard", "client"), P()),
        check_vma=False,
    )
```

profile of v0, /device:TPU:1, one launch (start us, length us, event | category | flops | bytes accessed | tf_op | source)
XLA Modules:
  0.0 173.4 jit_solution(2487355181392933128)
XLA Ops:
  7.2 0.0 reduce-scatter.4.cloned.1.call-start
  7.2 4.0 %fusion = f32[12]{0:T(128)S(1)} fusion(bf16[12,12,14336]{2,1,0:T(8,128)(2,1)} %param.7), kind=kLoop, calls=%fused_computation.2 | loop fusion | flops 6193140 | bytes 4128816 | tf_op jit(solution)/shard_map/reduce_sum | solution.py:41
  11.2 0.7 exp.3
  11.9 30.3 %psum.14 = f32[12]{0:T(128)S(1)} all-reduce(f32[12]{0:T(128)S(1)} %fusion), channel_id=1, replica_groups=mesh['client'=32,'shard'=16] {'shard'}, use_global_device_ids=true, to_apply=%region_2.0 | all-reduce | flops 12 | bytes 96 | tf_op jit(solution)/shard_map/psum | solution.py:46
  42.2 0.8 dynamic_slice.3
  43.0 0.2 select_reduce_fusion.1
  43.2 0.1 select_reduce_fusion
  43.3 4.0 %fusion.1 = f32[12,14336]{1,0:T(8,128)S(1)} fusion(bf16[12,12,14336]{2,1,0:T(8,128)(2,1)} %param.7, f32[12]{0:T(128)S(1)} %maximum_divide_fusion), kind=kLoop, calls=%fused_computation.3 | loop fusion | flops 6021120 | bytes 4816944 | tf_op jit(solution)/shard_map/reduce_sum | solution.py:50
  47.2 0.0 copy-start.1
  47.3 0.0 copy-start.2
  47.3 0.0 copy-start
  47.3 4.5 %copy.9 = f32[12,14336]{0,1:T(8,128)} copy(f32[12,14336]{1,0:T(8,128)S(1)} %fusion.1) | data formatting | bytes 1376256
  51.8 0.0 reduce-scatter.4.cloned.1.call-update
  51.8 70.0 %psum.15 = f32[12]{0:T(128)S(1)} all-reduce(f32[12]{0:T(128)S(1)} %select_reduce_fusion), channel_id=1, replica_groups=mesh['client'=32,'shard'=16] {'client'}, use_global_device_ids=true, to_apply=%region_9.10 | all-reduce | flops 12 | bytes 96 | tf_op jit(solution)/shard_map/psum | solution.py:48
  121.8 0.0 copy-done.1
  121.8 1.2 multiply_subtract_fusion
  125.0 0.2 reduce-window.8
  125.2 0.0 copy-done.2
  125.2 0.1 add_multiply_fusion
  125.3 0.2 fusion.10
  125.5 39.3 %reduce-scatter.4.cloned.1.call-done = f32[448,12]{1,0:T(8,128)} async-done(((f32[14336,12]{1,0:T(8,128)}), f32[448,12]{1,0:T(8,128)}) %reduce-scatter.4.cloned.1.call-update) | async-done | bytes 21520
  164.8 1.0 copy.10
  165.9 0.0 copy-done
  165.9 0.6 multiply_add_fusion
  (7 shorter events, 0.1 us)
Async XLA Ops:
  7.2 157.7 %reduce-scatter.4.cloned.1.call-start = ((), (), s32[]{:S(2)}) async-start(), calls=%async_computation.1 | async-start | bytes 7569408
  47.2 74.5 %copy-start.1 = (f32[12]{0:T(128)S(1)}, f32[12]{0:T(128)}, u32[]{:S(2)}) copy-start(f32[12]{0:T(128)} %param.9) | copy-start | bytes 148
  47.3 77.9 %copy-start.2 = (s32[8]{0:T(128)S(1)}, s32[8]{0:T(128)}, u32[]{:S(2)}) copy-start(s32[8]{0:T(128)} %param.11) | copy-start | bytes 100
  47.3 118.6 %copy-start = (f32[12,448]{1,0:T(8,128)S(1)}, f32[12,448]{1,0:T(8,128)}, u32[]{:S(2)}) copy-start(f32[12,448]{1,0:T(8,128)} %param.8) | copy-start | bytes 64516
Sparse Core Ops, SparseCore 0:
  51.9 112.8 reduce-scatter.3
where the time goes:
time: 174 us; the launch traced here: 173 us
  blocking collectives  100 us (57%)
  waiting for transfers between devices  39.3 us (23%)
  between operations  16.1 us (9%)
  other arithmetic  10.6 us (6%)
  local copies, waits for them, and re-layouts  6.99 us (4%)
    psum x1, blocking collectives, per_device(): counts = lax.psum(jnp.sum(own_member * own_bit[:, None], axis=0), 'client')  70 us
    unnamed x2, waiting for transfers between devices  39.3 us
    psum x1, blocking collectives, per_device(): norms = jnp.sqrt(lax.psum(squares, 'shard'))  30.3 us
    unnamed x8, local copies, waits for them, and re-layouts  5.58 us
    reduce_sum x1, other arithmetic, per_device(): squares = jnp.sum(jnp.square(updates.astype(jnp.float32)), axis=(1, 2))  4.01 us
    reduce_sum x1, other arithmetic, per_device(): jnp.sum(factor[:, None, None] * updates.astype(jnp.float32), axis=0)  3.98 us
  transfers between devices with their start and end apart: 1, of which 1 were waited for; matrix products, arithmetic and copies ran while one was open for 1% of the time, Pallas kernels for 0%

commit v1 on v0

v1 whole, which is shorter than its diff:
```python
import jax
import jax.numpy as jnp
from jax import lax
from jax.experimental import pallas as pl
from jax.experimental.pallas import tpu as pltpu
from jax.sharding import PartitionSpec as P

LANES = 128
MIB = 1024 * 1024


def mix(x):
    x = x ^ lax.shift_right_logical(x, jnp.int32(16))
    x = x * jnp.int32(2146121005)
    x = x ^ lax.shift_right_logical(x, jnp.int32(15))
    x = x * jnp.int32(-2073450869)
    x = x ^ lax.shift_right_logical(x, jnp.int32(16))
    return x


def lane_ids(shape):
    return lax.broadcasted_iota(jnp.int32, shape, len(shape) - 1)


def diagonal(size):
    return lax.broadcasted_iota(jnp.int32, (size, LANES), 0) == lane_ids((size, LANES))


EVEN = (0, 1, 2, 3)
ODD = (4, 5, 6, 3)
GROUPS = 7
SLAB = 6 * LANES
HALF = LANES // 2


def fold(x):
    parts = [x[:, at : at + LANES] for at in range(0, x.shape[1], LANES)]
    while len(parts) > 1:
        parts = [sum(parts[at : at + 2]) for at in range(0, len(parts), 2)]
    return parts[0]


def square_kernel(width, round_s, coef_s, log_hbm, cohort_hbm, seeds_hbm, momentum_hbm,
                  updates_hbm, held_ref, partial_ref, base_ref, log_ref, limit_ref, member_ref,
                  log_s, cohort_s, seeds_s, momentum_v, sums_v, small_sems, sems):
    local_clients, row_count, _ = held_ref.shape
    rows, cols = momentum_v.shape
    cohort_count = log_s.shape[0]
    total_clients = cohort_s.shape[0]
    small = []
    for k, (source, target) in enumerate((
        (seeds_hbm, seeds_s), (log_hbm, log_s), (cohort_hbm, cohort_s), (momentum_hbm, momentum_v),
    )):
        small.append(pltpu.make_async_copy(source, target, small_sems.at[k]))
        small[-1].start()
    for c in range(local_clients):
        pltpu.make_async_copy(updates_hbm.at[c], held_ref.at[c], sems.at[c]).start()
    for copy in small:
        copy.wait()

    lanes = lane_ids((1, LANES))
    own = lax.axis_index("client") * local_clients
    logs = jnp.full((1, LANES), log_s[0], jnp.float32)
    for g in range(1, cohort_count):
        logs = jnp.where(lanes == g, log_s[g], logs)
    log_ref[...] = logs
    largest = jnp.max(jnp.exp(logs), axis=1, keepdims=True)
    own_logs = jnp.zeros((1, LANES), jnp.float32)
    for c in range(local_clients):
        cohort = cohort_s[own + c]
        own_logs = jnp.where(lanes == c, log_s[cohort], own_logs)
        member_ref[c : c + 1, :] = jnp.where(lanes % HALF == cohort, 1.0, 0.0)
    limit_ref[...] = jnp.exp(own_logs)

    first_row = lax.axis_index("shard") * rows
    first_col = lax.axis_index("client") * cols
    row_ids = first_row + lax.broadcasted_iota(jnp.int32, (rows, cols), 0)
    col_ids = first_col + lax.broadcasted_iota(jnp.int32, (rows, cols), 1)
    spread = (row_ids * jnp.int32(width) + col_ids) * jnp.int32(1013904223)
    rate = 0.4 + 0.07 * jnp.full((1, 1), coef_s[0], jnp.int32).astype(jnp.float32)
    coef = jnp.ones((1, 1), jnp.float32)
    noise = jnp.zeros((rows, cols), jnp.float32)
    for j in range(seeds_s.shape[0]):
        if j:
            coef = coef * (rate * ((2.0 * j - 1.0) / (2.0 * j)))
        key = mix(seeds_s[j] ^ ((round_s[0] - j) * jnp.int32(1640531527)))
        hashed = mix(spread + key)
        uniform = (lax.shift_right_logical(hashed, jnp.int32(8)).astype(jnp.float32) + 0.5) * (
            1.0 / 16777216.0
        )
        noise = noise + coef * (3.4641016151377544 * (uniform - 0.5))
    base_ref[...] = 0.9 * momentum_v[...] + (0.05 * largest * noise) / total_clients

    step = 2 * GROUPS * LANES

    def add_client(c, carry):
        pltpu.make_async_copy(updates_hbm.at[c], held_ref.at[c], sems.at[c]).wait()
        acc = jnp.zeros((row_count, step), jnp.float32)
        for at in range(0, width, step):
            block = held_ref[c, :, at : at + step].astype(jnp.float32)
            acc = acc + block * block
        sums_v[c] = fold(acc)
        return carry

    lax.fori_loop(0, local_clients, add_client, 0)
    column = jnp.sum(jnp.sum(sums_v[...], axis=1), axis=1, keepdims=True)
    row = jnp.sum(jnp.where(diagonal(local_clients), column, 0.0), axis=0, keepdims=True)
    partial_ref[...] = jnp.broadcast_to(row[None], partial_ref.shape)


def weight_kernel(limit_ref, member_ref, squares_ref, held_ref, slab_ref):
    local_clients, row_count, width = held_ref.shape
    step = 2 * GROUPS * LANES
    norms = jnp.sqrt(jnp.sum(squares_ref[...], axis=0))
    limit = limit_ref[...]
    factor = limit / jnp.maximum(norms, limit)
    factors = [jnp.broadcast_to(factor[:, c : c + 1], (row_count, step)) for c in range(local_clients)]
    bit = (norms <= limit).astype(jnp.float32)
    bits = jnp.sum(jnp.where(diagonal(local_clients), bit, 0.0), axis=1, keepdims=True)
    counts = jnp.sum(member_ref[...] * bits, axis=0, keepdims=True)
    eight = (8, LANES)
    counts = jnp.where(lax.broadcasted_iota(jnp.int32, eight, 0) == 0, counts, 0.0)
    left = lane_ids(eight) < HALF

    def pairs(p, carry):
        at = pl.multiple_of(p * step, step)
        acc = jnp.zeros((row_count, step), jnp.float32)
        for c in range(local_clients):
            acc = acc + held_ref[c, :, pl.ds(at, step)].astype(jnp.float32) * factors[c]
        for k in range(4):
            def group(j, rows):
                first = ((k // 2) * GROUPS + j) * LANES
                return acc[rows, first : first + LANES]

            names = ODD if k % 2 else EVEN
            upper = [group(j, slice(0, 8)) for j in names]
            lower = [group(j, slice(8, 12)) for j in names]
            upper[3] = jnp.where(left, counts, upper[3]) if k % 2 else jnp.where(left, upper[3], counts)
            for j in range(4):
                slab_ref[4 * p + k, :, j * LANES : (j + 1) * LANES] = upper[j]
            for j in range(2):
                slab_ref[4 * p + k, :, (4 + j) * LANES : (5 + j) * LANES] = jnp.concatenate(
                    [lower[j], lower[j + 2]], axis=0
                )
        return carry

    lax.fori_loop(0, width // step, pairs, 0, unroll=2)


def own_columns(x, odd):
    as_odd = jnp.concatenate([x[:, 3 * LANES + HALF :], x[:, : 3 * LANES]], axis=1)
    return jnp.where(odd, as_odd, x[:, : 3 * LANES + HALF])


def finish_kernel(total_clients, cohort_count, log_ref, base_ref, slab_ref, momentum_ref, next_ref):
    odd = lax.axis_index("client") % 2 == 1
    total = jnp.sum(slab_ref[...], axis=0)
    upper = total[:, : 4 * LANES]
    lower = jnp.concatenate([total[:4, 4 * LANES :], total[4:, 4 * LANES :]], axis=1)
    momentum_ref[:8, :] = base_ref[:8, :] + own_columns(upper, odd) / total_clients
    momentum_ref[8:, :] = base_ref[8:, :] + own_columns(lower, odd) / total_clients
    middle = upper[:1, 3 * LANES :]
    counts = jnp.where(odd, middle[:, :cohort_count], middle[:, HALF : HALF + cohort_count])
    next_ref[...] = log_ref[:, :cohort_count] - 0.2 * (counts / (total_clients // cohort_count) - 0.5)


def per_device(updates, momentum, log_thresholds, cohort_of, seeds, round_index, coef_index):
    local_clients, _, width = updates.shape
    rows, cols = momentum.shape
    cohort_count = log_thresholds.shape[0]
    total_clients = cohort_of.shape[0]
    shards = lax.axis_size("shard")
    owners = lax.axis_size("client")
    vmem = pl.BlockSpec(memory_space=pltpu.VMEM)
    hbm = pl.BlockSpec(memory_space=pltpu.HBM)
    smem = pl.BlockSpec(memory_space=pltpu.SMEM)
    params = pltpu.CompilerParams(vmem_limit_bytes=24 * MIB)

    def square(*refs):
        square_kernel(width, *refs)

    held, partial, base, log_row, limit, member = pl.pallas_call(
        square,
        out_shape=(
            pltpu.VMEM(updates.shape, jnp.bfloat16),
            jax.ShapeDtypeStruct((shards, 1, LANES), jnp.float32),
            jax.ShapeDtypeStruct((rows, cols), jnp.float32),
            jax.ShapeDtypeStruct((1, LANES), jnp.float32),
            jax.ShapeDtypeStruct((1, LANES), jnp.float32),
            jax.ShapeDtypeStruct((local_clients, LANES), jnp.float32),
        ),
        in_specs=[smem] * 2 + [hbm] * 5,
        out_specs=(vmem,) * 6,
        scratch_shapes=[
            pltpu.SMEM((cohort_count,), jnp.float32),
            pltpu.SMEM((total_clients,), jnp.int32),
            pltpu.SMEM(seeds.shape, jnp.int32),
            pltpu.VMEM((rows, cols), jnp.float32),
            pltpu.VMEM((local_clients, rows, LANES), jnp.float32),
            pltpu.SemaphoreType.DMA((4,)),
            pltpu.SemaphoreType.DMA((local_clients,)),
        ],
        compiler_params=params,
        name="squares",
    )(round_index, coef_index, *(
        pltpu.with_memory_space_constraint(x, pltpu.HBM)
        for x in (log_thresholds, cohort_of, seeds, momentum, updates)
    ))

    squares = lax.all_to_all(partial, "shard", 0, 0, tiled=True)

    slabs = pl.pallas_call(
        weight_kernel,
        out_shape=jax.ShapeDtypeStruct((owners, 8, SLAB), jnp.float32),
        in_specs=[vmem] * 4,
        out_specs=vmem,
        compiler_params=params,
        name="weighted_sum",
    )(limit, member, squares, held)

    parts = lax.all_to_all(slabs, "client", 0, 0, tiled=True)

    def finish(*refs):
        finish_kernel(total_clients, cohort_count, *refs)

    momentum_next, log_next = pl.pallas_call(
        finish,
        out_shape=(
            jax.ShapeDtypeStruct((rows, cols), jnp.float32),
            jax.ShapeDtypeStruct((1, cohort_count), jnp.float32),
        ),
        in_specs=[vmem] * 3,
        out_specs=(vmem,) * 2,
        compiler_params=params,
        name="finish",
    )(log_row, base, parts)
    return (momentum_next, log_next.reshape(cohort_count))


def solution(mesh):
    placed = (P("client", "shard", None), P("shard", "client"), P(), P(), P(), P(), P())
    return jax.shard_map(
        per_device,
        mesh=mesh,
        in_specs=placed,
        out_specs=(P("shard", "client"), P()),
        check_vma=False,
    )
```

time: 174 us -> 57.8 us (0.33)
  blocking collectives: 100 us -> 50 us
  waiting for transfers between devices: 39.3 us -> 0 us
  between operations: 16.1 us -> 1.94 us
  other arithmetic: 10.6 us -> 0 us
  local copies, waits for them, and re-layouts: 6.99 us -> 0 us
  Pallas kernels: 0 us -> 5.66 us
    psum x2 -> x0, blocking collectives: 100 us -> none  [the longest x1 70 us: per_device(): counts = lax.psum(jnp.sum(own_member * own_bit[:, None], axis=0), 'client')]
    all_to_all x0 -> x2, blocking collectives: none -> 50 us  [the longest x1 26.8 us: per_device(): squares = lax.all_to_all(partial, 'shard', 0, 0, tiled=True)]
    unnamed x2 -> x0, waiting for transfers between devices: 39.3 us -> none
    reduce_sum x5 -> x0, other arithmetic: 8.48 us -> none  [the longest x1 4.01 us: per_device(): squares = jnp.sum(jnp.square(updates.astype(jnp.float32)), axis=(1, 2))]
    pallas_call x0 -> x3, Pallas kernels: none -> 5.66 us  [the longest x1 3.69 us: per_device(): pl.pallas_call(square, out_shape=(pltpu.VMEM(updates.shape, jnp.bfloat16)...]
    unnamed x8 -> x0, local copies, waits for them, and re-layouts: 5.58 us -> none
  transfers between devices with their start and end apart: 1 -> 0, of which waited for: 1 -> 0; matrix products, arithmetic and copies ran while one was open for 1% -> 0% of each run, Pallas kernels for 0% -> 0%
where the time goes in v1:
time: 57.8 us; the launch traced here: 57.6 us
  blocking collectives  50 us (87%)
  Pallas kernels  5.66 us (10%)
  between operations  1.94 us (3%)
    all_to_all x1, blocking collectives, per_device(): squares = lax.all_to_all(partial, 'shard', 0, 0, tiled=True)  26.8 us
    all_to_all x1, blocking collectives, per_device(): parts = lax.all_to_all(slabs, 'client', 0, 0, tiled=True)  23.2 us
    pallas_call x1, Pallas kernels, per_device(): pl.pallas_call(square, out_shape=(pltpu.VMEM(updates.shape, jnp.bfloat16)...  3.69 us
    pallas_call x1, Pallas kernels, per_device(): pl.pallas_call(weight_kernel, out_shape=jax.ShapeDtypeStruct((owners, 8,...  1.22 us

profile of v1, /device:TPU:1, one launch (start us, length us, event | category | flops | bytes accessed | tf_op | source)
XLA Modules:
  0.0 57.6 jit_solution(15218089318297485782)
XLA Ops:
  1.9 3.7 %squares.1 = (bf16[12,12,14336]{2,1,0:T(8,128)(2,1)S(1)}, f32[16,1,128]{2,1,0:T(1,128)S(1)}, f32[12,448]{1,0:T(8,128)S(1)}, f32[1,128]{1,0:T(1,128)S(1)}, f32[1,128]{1,0:T(1,128)S(1)}, /*index=5*/f32[12,128]{1,0:T(8,128)S(1)}) custom-call(s32[1]{0:T(128)S(6)} %copy.9.refs_0_, s32[1]{0:T(128)S(6)} %copy.10.refs_1_, f32[12]{0:T(128)} %refs_2_.1, s32[384]{0:T(512)} %refs_3_.1, ...), custom_call_target="tpu_custom_call" | custom-call | tf_op jit(solution)/shard_map/squares/pallas_call | solution.py:182
  5.6 26.8 %all_to_all.10.squares_ref = f32[16,1,128]{2,1,0:T(1,128)S(1)} all-to-all(f32[16,1,128]{2,1,0:T(1,128)S(1)} %get-tuple-element.14), channel_id=1, replica_groups=mesh['client'=32,'shard'=16] {'shard'}, dimensions={0} | all-to-all | bytes 16384 | tf_op jit(solution)/shard_map/all_to_all | solution.py:210
  32.5 1.2 %weighted_sum.1 = f32[32,8,768]{2,1,0:T(8,128)S(1)} custom-call(f32[1,128]{1,0:T(1,128)S(1)} %get-tuple-element.12.limit_ref, f32[12,128]{1,0:T(8,128)S(1)} %get-tuple-element.13.member_ref, f32[16,1,128]{2,1,0:T(1,128)S(1)} %all_to_all.10.squares_ref, bf16[12,12,14336]{2,1,0:T(8,128)(2,1)S(1)} %get-tuple-element.15.held_ref), custom_call_target="tpu_custom_call" | custom-call | tf_op jit(solution)/shard_map/weighted_sum/pallas_call | solution.py:212
  33.7 23.2 %all_to_all.11.refs_2_ = f32[32,8,768]{2,1,0:T(8,128)S(1)} all-to-all(f32[32,8,768]{2,1,0:T(8,128)S(1)} %weighted_sum.1), channel_id=1, replica_groups=mesh['client'=32,'shard'=16] {'client'}, dimensions={0} | all-to-all | bytes 1572864 | tf_op jit(solution)/shard_map/all_to_all | solution.py:221
  56.9 0.8 %finish.1 = (f32[12,448]{1,0:T(8,128)}, f32[1,12]{1,0:T(1,128)}) custom-call(f32[1,128]{1,0:T(1,128)S(1)} %get-tuple-element.10.refs_0_, f32[12,448]{1,0:T(8,128)S(1)} %get-tuple-element.11.refs_1_, f32[32,8,768]{2,1,0:T(8,128)S(1)} %all_to_all.11.refs_2_), custom_call_target="tpu_custom_call" | custom-call | tf_op jit(solution)/shard_map/finish/pallas_call | solution.py:226

commit v2 on v1

v2 whole, which is shorter than its diff:
```python
import jax
import jax.numpy as jnp
from jax import lax
from jax.experimental import pallas as pl
from jax.experimental.pallas import tpu as pltpu
from jax.sharding import PartitionSpec as P

LANES = 128
HALF = LANES // 2
MIB = 1024 * 1024

PAIR = 7 * LANES
REACH = 4 * LANES
SLAB = 6 * LANES


def mix(x):
    x = x ^ lax.shift_right_logical(x, jnp.int32(16))
    x = x * jnp.int32(2146121005)
    x = x ^ lax.shift_right_logical(x, jnp.int32(15))
    x = x * jnp.int32(-2073450869)
    x = x ^ lax.shift_right_logical(x, jnp.int32(16))
    return x


def lane_ids(shape):
    return lax.broadcasted_iota(jnp.int32, shape, len(shape) - 1)


def row_ids(shape):
    return lax.broadcasted_iota(jnp.int32, shape, len(shape) - 2)


def diagonal(size):
    return row_ids((size, LANES)) == lane_ids((size, LANES))


def fold(x):
    parts = [x[:, at : at + LANES] for at in range(0, x.shape[1], LANES)]
    while len(parts) > 1:
        parts = [sum(parts[at : at + 2]) for at in range(0, len(parts), 2)]
    return parts[0]


def square_kernel(log_hbm, cohort_hbm, seeds_hbm, momentum_hbm, updates_hbm,
                  held_ref, partial_ref, momentum_ref, seeds_ref, log_ref, limit_ref, member_ref,
                  log_s, cohort_s, seeds_s, sums_v, small_sems, sems):
    local_clients, row_count, width = held_ref.shape
    cohort_count = log_s.shape[0]
    small = []
    for k, (source, target) in enumerate((
        (log_hbm, log_s), (cohort_hbm, cohort_s), (seeds_hbm, seeds_s), (momentum_hbm, momentum_ref),
    )):
        small.append(pltpu.make_async_copy(source, target, small_sems.at[k]))
        small[-1].start()
    for c in range(local_clients):
        pltpu.make_async_copy(updates_hbm.at[c], held_ref.at[c], sems.at[c]).start()
    for copy in small:
        copy.wait()

    lanes = lane_ids((1, LANES))
    own = lax.axis_index("client") * local_clients
    logs = jnp.full((1, LANES), log_s[0], jnp.float32)
    for g in range(1, cohort_count):
        logs = jnp.where(lanes == g, log_s[g], logs)
    log_ref[...] = logs
    seed_row = jnp.zeros((1, LANES), jnp.int32)
    for j in range(seeds_s.shape[0]):
        seed_row = jnp.where(lanes == j, seeds_s[j], seed_row)
    seeds_ref[...] = seed_row
    own_logs = jnp.zeros((1, LANES), jnp.float32)
    for c in range(local_clients):
        cohort = cohort_s[own + c]
        own_logs = jnp.where(lanes == c, log_s[cohort], own_logs)
        member_ref[c : c + 1, :] = jnp.where((lanes & (HALF - 1)) == cohort, 1.0, 0.0)
    limit_ref[...] = jnp.exp(own_logs)

    step = 2 * PAIR

    def add_client(c, carry):
        pltpu.make_async_copy(updates_hbm.at[c], held_ref.at[c], sems.at[c]).wait()
        acc = jnp.zeros((row_count, step), jnp.float32)
        for at in range(0, width, step):
            block = held_ref[c, :, at : at + step].astype(jnp.float32)
            acc = acc + block * block
        sums_v[c] = fold(acc)
        return carry

    lax.fori_loop(0, local_clients, add_client, 0)
    column = jnp.sum(jnp.sum(sums_v[...], axis=1), axis=1, keepdims=True)
    row = jnp.sum(jnp.where(diagonal(local_clients), column, 0.0), axis=0, keepdims=True)
    partial_ref[...] = jnp.broadcast_to(row[None], partial_ref.shape)


def weight_kernel(other, limit_ref, member_ref, squares_ref, held_ref, slab_ref):
    local_clients, row_count, width = held_ref.shape
    odd = (lax.axis_index("client") + other) % 2
    norms = jnp.sqrt(jnp.sum(squares_ref[...], axis=0))
    limit = limit_ref[...]
    factor = limit / jnp.maximum(norms, limit)
    factors = [jnp.broadcast_to(factor[:, c : c + 1], (row_count, REACH)) for c in range(local_clients)]
    bit = (norms <= limit).astype(jnp.float32)
    bits = jnp.sum(jnp.where(diagonal(local_clients), bit, 0.0), axis=1, keepdims=True)
    counts = jnp.sum(member_ref[...] * bits, axis=0, keepdims=True)
    eight = (8, LANES)
    counts = jnp.where(row_ids(eight) == 0, counts, 0.0)
    left = lane_ids(eight) < HALF
    spare_first = left & (odd == 1)
    spare_last = jnp.logical_not(left) & (odd == 0)

    def pair(p, carry):
        at = pl.multiple_of(p * PAIR + odd * (PAIR - REACH), LANES)
        acc = jnp.zeros((row_count, REACH), jnp.float32)
        for c in range(local_clients):
            acc = acc + held_ref[c, :, pl.ds(at, REACH)].astype(jnp.float32) * factors[c]
        upper = [acc[:8, j * LANES : (j + 1) * LANES] for j in range(4)]
        lower = [acc[8:, j * LANES : (j + 1) * LANES] for j in range(4)]
        upper[0] = jnp.where(spare_first, counts, upper[0])
        upper[3] = jnp.where(spare_last, counts, upper[3])
        for j in range(4):
            slab_ref[p, :, j * LANES : (j + 1) * LANES] = upper[j]
        for j in range(2):
            slab_ref[p, :, (4 + j) * LANES : (5 + j) * LANES] = jnp.concatenate(
                [lower[j], lower[j + 2]], axis=0
            )
        return carry

    lax.fori_loop(0, width // PAIR, pair, 0, unroll=4)


def base_kernel(width, total_clients, band, round_s, coef_s, seeds_ref, log_ref, momentum_ref, base_ref):
    rows, cols = momentum_ref.shape
    first_row = lax.axis_index("shard") * rows
    first_col = lax.axis_index("client") * cols
    block = (rows, cols)
    index = (first_row + row_ids(block)) * jnp.int32(width) + (first_col + lane_ids(block))
    spread = index * jnp.int32(1013904223)
    keys = mix(seeds_ref[...] ^ ((round_s[0] - lane_ids((1, LANES))) * jnp.int32(1640531527)))
    rate = 0.4 + 0.07 * jnp.full((1, 1), coef_s[0], jnp.int32).astype(jnp.float32)
    coef = jnp.ones((1, 1), jnp.float32)
    noise = jnp.zeros(block, jnp.float32)
    for j in range(band):
        if j:
            coef = coef * (rate * ((2.0 * j - 1.0) / (2.0 * j)))
        hashed = mix(spread + keys[:, j : j + 1])
        uniform = (lax.shift_right_logical(hashed, jnp.int32(8)).astype(jnp.float32) + 0.5) * (
            1.0 / 16777216.0
        )
        noise = noise + coef * (3.4641016151377544 * (uniform - 0.5))
    largest = jnp.max(jnp.exp(log_ref[...]), axis=1, keepdims=True)
    base_ref[...] = 0.9 * momentum_ref[...] + (0.05 * largest * noise) / total_clients


def finish_kernel(total_clients, cohort_count, log_ref, base_ref, slab_ref, momentum_ref, next_ref):
    cols = base_ref.shape[1]
    odd = lax.axis_index("client") % 2 == 1
    total = jnp.sum(slab_ref[...], axis=0)
    upper = total[:, :REACH]
    lower = jnp.concatenate([total[:4, REACH:], total[4:, REACH:]], axis=1)
    upper_own = jnp.where(odd, upper[:, HALF:], upper[:, :cols])
    lower_own = jnp.where(odd, lower[:, HALF:], lower[:, :cols])
    momentum_ref[:8, :] = base_ref[:8, :] + upper_own / total_clients
    momentum_ref[8:, :] = base_ref[8:, :] + lower_own / total_clients
    counts = jnp.where(odd, upper[:1, :cohort_count], upper[:1, cols : cols + cohort_count])
    next_ref[...] = log_ref[:, :cohort_count] - 0.2 * (counts / (total_clients // cohort_count) - 0.5)


def per_device(updates, momentum, log_thresholds, cohort_of, seeds, round_index, coef_index):
    local_clients, _, width = updates.shape
    rows, cols = momentum.shape
    cohort_count = log_thresholds.shape[0]
    total_clients = cohort_of.shape[0]
    shards = lax.axis_size("shard")
    owners = lax.axis_size("client")
    chips = owners // 2
    vmem = pl.BlockSpec(memory_space=pltpu.VMEM)
    hbm = pl.BlockSpec(memory_space=pltpu.HBM)
    smem = pl.BlockSpec(memory_space=pltpu.SMEM)
    params = pltpu.CompilerParams(vmem_limit_bytes=24 * MIB)
    row = jax.ShapeDtypeStruct((1, LANES), jnp.float32)

    held, partial, momentum_v, seed_row, log_row, limit, member = pl.pallas_call(
        square_kernel,
        out_shape=(
            pltpu.VMEM(updates.shape, jnp.bfloat16),
            jax.ShapeDtypeStruct((shards, 1, LANES), jnp.float32),
            pltpu.VMEM((rows, cols), jnp.float32),
            jax.ShapeDtypeStruct((1, LANES), jnp.int32),
            row,
            row,
            jax.ShapeDtypeStruct((local_clients, LANES), jnp.float32),
        ),
        in_specs=[hbm] * 5,
        out_specs=(vmem,) * 7,
        scratch_shapes=[
            pltpu.SMEM((cohort_count,), jnp.float32),
            pltpu.SMEM((total_clients,), jnp.int32),
            pltpu.SMEM(seeds.shape, jnp.int32),
            pltpu.VMEM((local_clients, rows, LANES), jnp.float32),
            pltpu.SemaphoreType.DMA((4,)),
            pltpu.SemaphoreType.DMA((local_clients,)),
        ],
        compiler_params=params,
        name="squares",
    )(*(
        pltpu.with_memory_space_constraint(x, pltpu.HBM)
        for x in (log_thresholds, cohort_of, seeds, momentum, updates)
    ))

    squares = lax.all_to_all(partial, "shard", 0, 0, tiled=True)

    def weighted(other):
        def weight(*refs):
            weight_kernel(other, *refs)

        return pl.pallas_call(
            weight,
            out_shape=jax.ShapeDtypeStruct((chips, 8, SLAB), jnp.float32),
            in_specs=[vmem] * 4,
            out_specs=vmem,
            compiler_params=params,
            cost_estimate=pl.CostEstimate(
                flops=2 * updates.size, bytes_accessed=updates.size, transcendentals=0
            ),
            name="weighted_theirs" if other else "weighted_own",
        )(limit, member, squares, held)

    theirs = weighted(1)
    theirs, round_index, coef_index = lax.optimization_barrier((theirs, round_index, coef_index))
    arrived = lax.ppermute(theirs, "client", [(i, i ^ 1) for i in range(owners)])
    own = weighted(0)

    def base_of(*refs):
        base_kernel(width, total_clients, seeds.shape[0], *refs)

    base = pl.pallas_call(
        base_of,
        out_shape=jax.ShapeDtypeStruct((rows, cols), jnp.float32),
        in_specs=[smem] * 2 + [vmem] * 3,
        out_specs=vmem,
        compiler_params=params,
        cost_estimate=pl.CostEstimate(
            flops=200 * momentum.size, bytes_accessed=8 * momentum.size, transcendentals=0
        ),
        name="base",
    )(round_index, coef_index, seed_row, log_row, momentum_v)

    parts = lax.all_to_all(
        own + arrived, "client", 0, 0, tiled=True,
        axis_index_groups=[[2 * i + core for i in range(chips)] for core in range(2)],
    )

    def finish(*refs):
        finish_kernel(total_clients, cohort_count, *refs)

    momentum_next, log_next = pl.pallas_call(
        finish,
        out_shape=(
            jax.ShapeDtypeStruct((rows, cols), jnp.float32),
            jax.ShapeDtypeStruct((1, cohort_count), jnp.float32),
        ),
        in_specs=[vmem] * 3,
        out_specs=(vmem,) * 2,
        compiler_params=params,
        name="finish",
    )(log_row, base, parts)
    return (momentum_next, log_next.reshape(cohort_count))


def solution(mesh):
    placed = (P("client", "shard", None), P("shard", "client"), P(), P(), P(), P(), P())
    return jax.shard_map(
        per_device,
        mesh=mesh,
        in_specs=placed,
        out_specs=(P("shard", "client"), P()),
        check_vma=False,
    )
```

time: 57.8 us -> 55 us (0.952)
  blocking collectives: 50 us -> 26.8 us
  starting transfers between devices: 0 us -> 10.8 us
  waiting for transfers between devices: 0 us -> 8.26 us
  other arithmetic: 0 us -> 0.8 us
    all_to_all x1 -> x0, blocking collectives: 23.2 us -> none  [per_device(): parts = lax.all_to_all(slabs, 'client', 0, 0, tiled=True)]
    all_to_all x0 -> x1, waiting for transfers between devices: none -> 7.7 us  [per_device(): lax.all_to_all(own + arrived, 'client', 0, 0, tiled=True, axis_index_grou...]
    all_to_all x0 -> x1, starting transfers between devices: none -> 6.75 us  [per_device(): lax.all_to_all(own + arrived, 'client', 0, 0, tiled=True, axis_index_grou...]
    ppermute x0 -> x1, starting transfers between devices: none -> 4 us  [per_device(): lax.ppermute(theirs, 'client', [(i, i ^ 1) for i in range(owners)])]
    add x0 -> x1, other arithmetic: none -> 0.8 us  [per_device(): own + arrived]
    pallas_call x2 -> x4, Pallas kernels: 4.91 us -> 5.27 us  [the longest x1 3.52 us: per_device(): pl.pallas_call(square_kernel, out_shape=(pltpu.VMEM(updates.shape, jnp.bf...]
  transfers between devices with their start and end apart: 0 -> 2, of which waited for: 0 -> 2; matrix products, arithmetic and copies ran while one was open for 0% -> 0% of each run, Pallas kernels for 0% -> 2%
where the time goes in v2:
time: 55 us; the launch traced here: 54.7 us
  blocking collectives  26.8 us (49%)
  starting transfers between devices  10.8 us (20%)
  waiting for transfers between devices  8.26 us (15%)
  Pallas kernels  6.06 us (11%)
  between operations  1.97 us (4%)
  other arithmetic  0.8 us (1%)
    all_to_all x1, blocking collectives, per_device(): squares = lax.all_to_all(partial, 'shard', 0, 0, tiled=True)  26.8 us
    all_to_all x1, waiting for transfers between devices, per_device(): lax.all_to_all(own + arrived, 'client', 0, 0, tiled=True, axis_index_grou...  7.7 us
    all_to_all x1, starting transfers between devices, per_device(): lax.all_to_all(own + arrived, 'client', 0, 0, tiled=True, axis_index_grou...  6.75 us
    ppermute x1, starting transfers between devices, per_device(): lax.ppermute(theirs, 'client', [(i, i ^ 1) for i in range(owners)])  4 us
    pallas_call x1, Pallas kernels, per_device(): pl.pallas_call(square_kernel, out_shape=(pltpu.VMEM(updates.shape, jnp.bf...  3.52 us
    pallas_call x2, Pallas kernels, weighted(): pl.pallas_call(weight, out_shape=jax.ShapeDtypeStruct((chips, 8, SLAB), j...  1.52 us
  transfers between devices with their start and end apart: 2, of which 2 were waited for; matrix products, arithmetic and copies ran while one was open for 0% of the time, Pallas kernels for 2%

profile of v2, /device:TPU:1, one launch (start us, length us, event | category | flops | bytes accessed | tf_op | source)
XLA Modules:
  0.0 54.7 jit_solution(1435642347211764110)
XLA Ops:
  0.6 3.5 %squares.1 = (bf16[12,12,14336]{2,1,0:T(8,128)(2,1)S(1)}, f32[16,1,128]{2,1,0:T(1,128)S(1)}, f32[12,448]{1,0:T(8,128)S(1)}, s32[1,128]{1,0:T(1,128)S(1)}, f32[1,...) custom-call(f32[12]{0:T(128)} %log_hbm.1, s32[384]{0:T(512)} %cohort_hbm.1, s32[8]{0:T(128)} %seeds_hbm.1, ...), custom_call_target="tpu_custom_call" | custom-call | tf_op jit(solution)/shard_map/squares/pallas_call | solution.py:182
  4.2 26.8 %all_to_all.10.refs_2_ = f32[16,1,128]{2,1,0:T(1,128)S(1)} all-to-all(f32[16,1,128]{2,1,0:T(1,128)S(1)} %get-tuple-element.17), channel_id=1, replica_groups=mesh['client'=32,'shard'=16] {'shard'}, dimensions={0} | all-to-all | bytes 16384 | tf_op jit(solution)/shard_map/all_to_all | solution.py:210
  31.0 0.8 %weighted_theirs.1 = f32[16,8,768]{2,1,0:T(8,128)S(1)} custom-call(f32[1,128]{1,0:T(1,128)S(1)} %get-tuple-element.15.refs_0_, f32[12,128]{1,0:T(8,128)S(1)} %get-tuple-element.16.refs_1_, f32[16,1,128]{2,1,0:T(1,128)S(1)} %all_to_all.10.refs_2_, bf16[12,12,14336]{2,1,0:T(8,128)(2,1)S(1)} %get-tuple-element.18.refs_3_), custom_call_target="tpu_custom_call" | custom-call | flops 4128768 | bytes 2064384 | tf_op jit(solution)/shard_map/weighted_theirs/pallas_call | solution.py:216
  31.8 4.0 %collective-permute-start = (f32[16,8,768]{2,1,0:T(8,128)S(1)}, f32[16,8,768]{2,1,0:T(8,128)S(1)}, u32[]{:S(2)}, u32[]{:S(2)}) collective-permute-start(f32[16,8,768]{2,1,0:T(8,128)S(1)} %weighted_theirs.1), channel_id=1, source_target_pairs={{0,16},{16,0},{32,48},{48,32},{64,80},{80,64},{96,112},{112,96},{1... | collective-permute-start | bytes 1179656 | tf_op jit(solution)/shard_map/ppermute | solution.py:230
  35.8 0.8 %weighted_own.1 = f32[16,8,768]{2,1,0:T(8,128)S(1)} custom-call(f32[1,128]{1,0:T(1,128)S(1)} %get-tuple-element.15.refs_0_, f32[12,128]{1,0:T(8,128)S(1)} %get-tuple-element.16.refs_1_, f32[16,1,128]{2,1,0:T(1,128)S(1)} %all_to_all.10.refs_2_, bf16[12,12,14336]{2,1,0:T(8,128)(2,1)S(1)} %get-tuple-element.18.refs_3_), custom_call_target="tpu_custom_call" | custom-call | flops 4128768 | bytes 2064384 | tf_op jit(solution)/shard_map/weighted_own/pallas_call | solution.py:216
  36.5 0.6 %collective-permute-done = f32[16,8,768]{2,1,0:T(8,128)S(1)} collective-permute-done((f32[16,8,768]{2,1,0:T(8,128)S(1)}, f32[16,8,768]{2,1,0:T(8,128)S(1)}, u32[]{:S(2)}, u32[]{:S(2)}) %collective-permute-start) | collective-permute-done | bytes 393248 | tf_op jit(solution)/shard_map/ppermute | solution.py:230
  37.1 0.8 %add.3 = f32[16,8,768]{2,1,0:T(8,128)} add(f32[16,8,768]{2,1,0:T(8,128)S(1)} %weighted_own.1, f32[16,8,768]{2,1,0:T(8,128)S(1)} %collective-permute-done) | non-fusion elementwise | flops 98304 | bytes 1179648 | tf_op jit(solution)/shard_map/add | solution.py:249
  37.9 6.8 %all-to-all-start.1 = ((f32[16,8,768]{2,1,0:T(8,128)}), f32[16,8,768]{2,1,0:T(8,128)S(1)}, u32[]{:S(2)}, u32[]{:S(2)}) async-start(f32[16,8,768]{2,1,0:T(8,128)} %add.3), calls=%async_computation.1 | async-start | bytes 786432 | tf_op jit(solution)/shard_map/all_to_all | solution.py:248
  46.0 0.2 base.1.refs_1_
  46.2 7.7 %all-to-all-done.1.refs_2_ = f32[16,8,768]{2,1,0:T(8,128)S(1)} async-done(((f32[16,8,768]{2,1,0:T(8,128)}), f32[16,8,768]{2,1,0:T(8,128)S(1)}, u32[]{:S(2)}, u32[]{:S(2)}) %all-to-all-start.1) | async-done | bytes 393248 | tf_op jit(solution)/shard_map/all_to_all | solution.py:248
  53.9 0.8 %finish.1 = (f32[12,448]{1,0:T(8,128)}, f32[1,12]{1,0:T(1,128)}) custom-call(f32[1,128]{1,0:T(1,128)S(1)} %get-tuple-element.14.refs_3_.refs_0_, f32[12,448]{1,0:T(8,128)S(1)} %base.1.refs_1_, f32[16,8,768]{2,1,0:T(8,128)S(1)} %all-to-all-done.1.refs_2_), custom_call_target="tpu_custom_call" | custom-call | tf_op jit(solution)/shard_map/finish/pallas_call | solution.py:256
Async XLA Ops:
  31.8 5.3 %collective-permute-start = (f32[16,8,768]{2,1,0:T(8,128)S(1)}, f32[16,8,768]{2,1,0:T(8,128)S(1)}, u32[]{:S(2)}, u32[]{:S(2)}) collective-permute-start(f32[16,8,768]{2,1,0:T(8,128)S(1)} %weighted_theirs.1), channel_id=1, source_target_pairs={{0,16},{16,0},{32,48},{48,32},{64,80},{80,64},{96,112},{112,96},{1... | collective-permute-start | bytes 1179656 | tf_op jit(solution)/shard_map/ppermute | solution.py:230
  37.9 16.0 %all-to-all-start.1 = ((f32[16,8,768]{2,1,0:T(8,128)}), f32[16,8,768]{2,1,0:T(8,128)S(1)}, u32[]{:S(2)}, u32[]{:S(2)}) async-start(f32[16,8,768]{2,1,0:T(8,128)} %add.3), calls=%async_computation.1 | async-start | bytes 786432 | tf_op jit(solution)/shard_map/all_to_all | solution.py:248

commit v3 on v2

--- a/solution.py
+++ b/solution.py
@@ -3,7 +3,7 @@
 from jax import lax
 from jax.experimental import pallas as pl
 from jax.experimental.pallas import tpu as pltpu
-from jax.sharding import PartitionSpec as P
+from jax.sharding import Mesh, PartitionSpec as P
 
 LANES = 128
 HALF = LANES // 2
@@ -59,7 +59,7 @@
         copy.wait()
 
     lanes = lane_ids((1, LANES))
-    own = lax.axis_index("client") * local_clients
+    own = (2 * lax.axis_index("chip") + lax.axis_index("core")) * local_clients
     logs = jnp.full((1, LANES), log_s[0], jnp.float32)
     for g in range(1, cohort_count):
         logs = jnp.where(lanes == g, log_s[g], logs)
@@ -94,7 +94,7 @@
 
 def weight_kernel(other, limit_ref, member_ref, squares_ref, held_ref, slab_ref):
     local_clients, row_count, width = held_ref.shape
-    odd = (lax.axis_index("client") + other) % 2
+    odd = (lax.axis_index("core") + other) % 2
     norms = jnp.sqrt(jnp.sum(squares_ref[...], axis=0))
     limit = limit_ref[...]
     factor = limit / jnp.maximum(norms, limit)
@@ -131,7 +131,7 @@
 def base_kernel(width, total_clients, band, round_s, coef_s, seeds_ref, log_ref, momentum_ref, base_ref):
     rows, cols = momentum_ref.shape
     first_row = lax.axis_index("shard") * rows
-    first_col = lax.axis_index("client") * cols
+    first_col = (2 * lax.axis_index("chip") + lax.axis_index("core")) * cols
     block = (rows, cols)
     index = (first_row + row_ids(block)) * jnp.int32(width) + (first_col + lane_ids(block))
     spread = index * jnp.int32(1013904223)
@@ -151,9 +151,13 @@
     base_ref[...] = 0.9 * momentum_ref[...] + (0.05 * largest * noise) / total_clients
 
 
+def add_kernel(one_ref, other_ref, sum_ref):
+    sum_ref[...] = one_ref[...] + other_ref[...]
+
+
 def finish_kernel(total_clients, cohort_count, log_ref, base_ref, slab_ref, momentum_ref, next_ref):
     cols = base_ref.shape[1]
-    odd = lax.axis_index("client") % 2 == 1
+    odd = lax.axis_index("core") == 1
     total = jnp.sum(slab_ref[...], axis=0)
     upper = total[:, :REACH]
     lower = jnp.concatenate([total[:4, REACH:], total[4:, REACH:]], axis=1)
@@ -171,8 +175,7 @@
     cohort_count = log_thresholds.shape[0]
     total_clients = cohort_of.shape[0]
     shards = lax.axis_size("shard")
-    owners = lax.axis_size("client")
-    chips = owners // 2
+    chips = lax.axis_size("chip")
     vmem = pl.BlockSpec(memory_space=pltpu.VMEM)
     hbm = pl.BlockSpec(memory_space=pltpu.HBM)
     smem = pl.BlockSpec(memory_space=pltpu.SMEM)
@@ -207,7 +210,10 @@
         for x in (log_thresholds, cohort_of, seeds, momentum, updates)
     ))
 
-    squares = lax.all_to_all(partial, "shard", 0, 0, tiled=True)
+    partial, round_index, coef_index = lax.optimization_barrier((partial, round_index, coef_index))
+    squares = lax.all_to_all(
+        partial, "shard", 0, 0, tiled=True, axis_index_groups=[list(range(shards))]
+    )
 
     def weighted(other):
         def weight(*refs):
@@ -226,8 +232,7 @@
         )(limit, member, squares, held)
 
     theirs = weighted(1)
-    theirs, round_index, coef_index = lax.optimization_barrier((theirs, round_index, coef_index))
-    arrived = lax.ppermute(theirs, "client", [(i, i ^ 1) for i in range(owners)])
+    arrived = lax.ppermute(theirs, "core", [(0, 1), (1, 0)])
     own = weighted(0)
 
     def base_of(*refs):
@@ -245,10 +250,15 @@
         name="base",
     )(round_index, coef_index, seed_row, log_row, momentum_v)
 
-    parts = lax.all_to_all(
-        own + arrived, "client", 0, 0, tiled=True,
-        axis_index_groups=[[2 * i + core for i in range(chips)] for core in range(2)],
-    )
+    both = pl.pallas_call(
+        add_kernel,
+        out_shape=jax.ShapeDtypeStruct(own.shape, jnp.float32),
+        in_specs=[vmem] * 2,
+        out_specs=vmem,
+        compiler_params=params,
+        name="add_cores",
+    )(own, arrived)
+    parts = lax.all_to_all(both, "chip", 0, 0, tiled=True)
 
     def finish(*refs):
         finish_kernel(total_clients, cohort_count, *refs)
@@ -268,11 +278,13 @@
 
 
 def solution(mesh):
-    placed = (P("client", "shard", None), P("shard", "client"), P(), P(), P(), P(), P())
+    clients, shards = mesh.devices.shape
+    split = Mesh(mesh.devices.reshape(clients // 2, 2, shards), ("chip", "core", "shard"))
+    client = ("chip", "core")
     return jax.shard_map(
         per_device,
-        mesh=mesh,
-        in_specs=placed,
-        out_specs=(P("shard", "client"), P()),
+        mesh=split,
+        in_specs=(P(client, "shard", None), P("shard", client), P(), P(), P(), P(), P()),
+        out_specs=(P("shard", client), P()),
         check_vma=False,
     )

time: 55 us -> 55 us (level)
  other arithmetic: 0.8 us -> 0 us
  Pallas kernels: 6.06 us -> 6.85 us
    add x1 -> x0, other arithmetic: 0.8 us -> none  [per_device(): own + arrived]
    pallas_call x0 -> x1, Pallas kernels: none -> 0.79 us  [per_device(): pl.pallas_call(add_kernel, out_shape=jax.ShapeDtypeStruct(own.shape, jnp....]
where the time goes in v3:
time: 55 us; the launch traced here: 54.7 us
  blocking collectives  26.8 us (49%)
  starting transfers between devices  10.8 us (20%)
  waiting for transfers between devices  8.26 us (15%)
  Pallas kernels  6.85 us (12%)
  between operations  1.97 us (4%)
    all_to_all x1, blocking collectives, per_device(): lax.all_to_all(partial, 'shard', 0, 0, tiled=True, axis_index_groups=[lis...  26.8 us
    all_to_all x1, waiting for transfers between devices, per_device(): parts = lax.all_to_all(both, 'chip', 0, 0, tiled=True)  7.7 us
    all_to_all x1, starting transfers between devices, per_device(): parts = lax.all_to_all(both, 'chip', 0, 0, tiled=True)  6.75 us
    ppermute x1, starting transfers between devices, per_device(): arrived = lax.ppermute(theirs, 'core', [(0, 1), (1, 0)])  4 us
    pallas_call x1, Pallas kernels, per_device(): pl.pallas_call(square_kernel, out_shape=(pltpu.VMEM(updates.shape, jnp.bf...  3.52 us
    pallas_call x2, Pallas kernels, weighted(): pl.pallas_call(weight, out_shape=jax.ShapeDtypeStruct((chips, 8, SLAB), j...  1.52 us
  transfers between devices with their start and end apart: 2, of which 2 were waited for; matrix products, arithmetic and copies ran while one was open for 0% of the time, Pallas kernels for 2%

profile of v3, /device:TPU:1, one launch (start us, length us, event | category | flops | bytes accessed | tf_op | source)
XLA Modules:
  0.0 54.7 jit_solution(16865602043992787600)
XLA Ops:
  0.6 3.5 %squares.1 = (bf16[12,12,14336]{2,1,0:T(8,128)(2,1)S(1)}, f32[16,1,128]{2,1,0:T(1,128)S(1)}, f32[12,448]{1,0:T(8,128)S(1)}, s32[1,128]{1,0:T(1,128)S(1)}, f32[1,...) custom-call(f32[12]{0:T(128)} %log_hbm.1, s32[384]{0:T(512)} %cohort_hbm.1, s32[8]{0:T(128)} %seeds_hbm.1, ...), custom_call_target="tpu_custom_call" | custom-call | tf_op jit(solution)/shard_map/squares/pallas_call | solution.py:185
  4.2 26.8 %all_to_all.10.refs_2_ = f32[16,1,128]{2,1,0:T(1,128)S(1)} all-to-all(f32[16,1,128]{2,1,0:T(1,128)S(1)} %get-tuple-element.22), channel_id=1, replica_groups={{0,1,2,3,4,5,6,7,8,9,10,11,12,13,14,15},{16,17,18,19,20,21,22,23,24,25,..., dimensions={0} | all-to-all | bytes 16384 | tf_op jit(solution)/shard_map/all_to_all | solution.py:214
  31.0 0.8 %weighted_theirs.1 = f32[16,8,768]{2,1,0:T(8,128)S(1)} custom-call(f32[1,128]{1,0:T(1,128)S(1)} %get-tuple-element.20.refs_0_, f32[12,128]{1,0:T(8,128)S(1)} %get-tuple-element.21.refs_1_, f32[16,1,128]{2,1,0:T(1,128)S(1)} %all_to_all.10.refs_2_, bf16[12,12,14336]{2,1,0:T(8,128)(2,1)S(1)} %get-tuple-element.23.refs_3_), custom_call_target="tpu_custom_call" | custom-call | flops 4128768 | bytes 2064384 | tf_op jit(solution)/shard_map/weighted_theirs/pallas_call | solution.py:222
  31.8 4.0 %collective-permute-start = (f32[16,8,768]{2,1,0:T(8,128)S(1)}, f32[16,8,768]{2,1,0:T(8,128)S(1)}, u32[]{:S(2)}, u32[]{:S(2)}) collective-permute-start(f32[16,8,768]{2,1,0:T(8,128)S(1)} %weighted_theirs.1), channel_id=1, source_target_pairs={{0,16},{16,0},{1,17},{17,1},{2,18},{18,2},{3,19},{19,3},{4,20},{20... | collective-permute-start | bytes 1179656 | tf_op jit(solution)/shard_map/ppermute | solution.py:235
  35.8 0.8 %weighted_own.1.one_ref = f32[16,8,768]{2,1,0:T(8,128)S(1)} custom-call(f32[1,128]{1,0:T(1,128)S(1)} %get-tuple-element.20.refs_0_, f32[12,128]{1,0:T(8,128)S(1)} %get-tuple-element.21.refs_1_, f32[16,1,128]{2,1,0:T(1,128)S(1)} %all_to_all.10.refs_2_, bf16[12,12,14336]{2,1,0:T(8,128)(2,1)S(1)} %get-tuple-element.23.refs_3_), custom_call_target="tpu_custom_call" | custom-call | flops 4128768 | bytes 2064384 | tf_op jit(solution)/shard_map/weighted_own/pallas_call | solution.py:222
  36.5 0.6 %collective-permute-done.other_ref = f32[16,8,768]{2,1,0:T(8,128)S(1)} collective-permute-done((f32[16,8,768]{2,1,0:T(8,128)S(1)}, f32[16,8,768]{2,1,0:T(8,128)S(1)}, u32[]{:S(2)}, u32[]{:S(2)}) %collective-permute-start) | collective-permute-done | bytes 393248 | tf_op jit(solution)/shard_map/ppermute | solution.py:235
  37.1 0.8 %add_cores.1 = f32[16,8,768]{2,1,0:T(8,128)} custom-call(f32[16,8,768]{2,1,0:T(8,128)S(1)} %weighted_own.1.one_ref, f32[16,8,768]{2,1,0:T(8,128)S(1)} %collective-permute-done.other_ref), custom_call_target="tpu_custom_call" | custom-call | tf_op jit(solution)/shard_map/add_cores/pallas_call | solution.py:253
  37.9 6.8 %all-to-all-start.1 = ((f32[16,8,768]{2,1,0:T(8,128)}), f32[16,8,768]{2,1,0:T(8,128)S(1)}, u32[]{:S(2)}, u32[]{:S(2)}) async-start(f32[16,8,768]{2,1,0:T(8,128)} %add_cores.1), calls=%async_computation.1 | async-start | bytes 786432 | tf_op jit(solution)/shard_map/all_to_all | solution.py:261
  45.9 0.2 base.1.refs_1_
  46.2 7.7 %all-to-all-done.1.refs_2_ = f32[16,8,768]{2,1,0:T(8,128)S(1)} async-done(((f32[16,8,768]{2,1,0:T(8,128)}), f32[16,8,768]{2,1,0:T(8,128)S(1)}, u32[]{:S(2)}, u32[]{:S(2)}) %all-to-all-start.1) | async-done | bytes 393248 | tf_op jit(solution)/shard_map/all_to_all | solution.py:261
  53.9 0.8 %finish.1 = (f32[12,448]{1,0:T(8,128)}, f32[1,12]{1,0:T(1,128)}) custom-call(f32[1,128]{1,0:T(1,128)S(1)} %get-tuple-element.14.refs_3_.refs_0_, f32[12,448]{1,0:T(8,128)S(1)} %base.1.refs_1_, f32[16,8,768]{2,1,0:T(8,128)S(1)} %all-to-all-done.1.refs_2_), custom_call_target="tpu_custom_call" | custom-call | tf_op jit(solution)/shard_map/finish/pallas_call | solution.py:266
Async XLA Ops:
  31.8 5.3 %collective-permute-start = (f32[16,8,768]{2,1,0:T(8,128)S(1)}, f32[16,8,768]{2,1,0:T(8,128)S(1)}, u32[]{:S(2)}, u32[]{:S(2)}) collective-permute-start(f32[16,8,768]{2,1,0:T(8,128)S(1)} %weighted_theirs.1), channel_id=1, source_target_pairs={{0,16},{16,0},{1,17},{17,1},{2,18},{18,2},{3,19},{19,3},{4,20},{20... | collective-permute-start | bytes 1179656 | tf_op jit(solution)/shard_map/ppermute | solution.py:235
  37.9 16.0 %all-to-all-start.1 = ((f32[16,8,768]{2,1,0:T(8,128)}), f32[16,8,768]{2,1,0:T(8,128)S(1)}, u32[]{:S(2)}, u32[]{:S(2)}) async-start(f32[16,8,768]{2,1,0:T(8,128)} %add_cores.1), calls=%async_computation.1 | async-start | bytes 786432 | tf_op jit(solution)/shard_map/all_to_all | solution.py:261

commit v4 on v3

--- a/solution.py
+++ b/solution.py
@@ -215,6 +215,21 @@
         partial, "shard", 0, 0, tiled=True, axis_index_groups=[list(range(shards))]
     )
 
+    def base_of(*refs):
+        base_kernel(width, total_clients, seeds.shape[0], *refs)
+
+    base = pl.pallas_call(
+        base_of,
+        out_shape=jax.ShapeDtypeStruct((rows, cols), jnp.float32),
+        in_specs=[smem] * 2 + [vmem] * 3,
+        out_specs=vmem,
+        compiler_params=params,
+        cost_estimate=pl.CostEstimate(
+            flops=200 * momentum.size, bytes_accessed=8 * momentum.size, transcendentals=0
+        ),
+        name="base",
+    )(round_index, coef_index, seed_row, log_row, momentum_v)
+
     def weighted(other):
         def weight(*refs):
             weight_kernel(other, *refs)
@@ -235,21 +250,6 @@
     arrived = lax.ppermute(theirs, "core", [(0, 1), (1, 0)])
     own = weighted(0)
 
-    def base_of(*refs):
-        base_kernel(width, total_clients, seeds.shape[0], *refs)
-
-    base = pl.pallas_call(
-        base_of,
-        out_shape=jax.ShapeDtypeStruct((rows, cols), jnp.float32),
-        in_specs=[smem] * 2 + [vmem] * 3,
-        out_specs=vmem,
-        compiler_params=params,
-        cost_estimate=pl.CostEstimate(
-            flops=200 * momentum.size, bytes_accessed=8 * momentum.size, transcendentals=0
-        ),
-        name="base",
-    )(round_index, coef_index, seed_row, log_row, momentum_v)
-
     both = pl.pallas_call(
         add_kernel,
         out_shape=jax.ShapeDtypeStruct(own.shape, jnp.float32),
@@ -258,6 +258,7 @@
         compiler_params=params,
         name="add_cores",
     )(own, arrived)
+    both, base = lax.optimization_barrier((both, base))
     parts = lax.all_to_all(both, "chip", 0, 0, tiled=True)
 
     def finish(*refs):

time: 55 us -> 54.8 us (level)
  blocking collectives: 26.8 us -> 42.5 us
  waiting for transfers between devices: 8.26 us -> 0.01 us
  starting transfers between devices: 10.8 us -> 4 us
  Pallas kernels: 6.85 us -> 6.1 us
    all_to_all x0 -> x1, blocking collectives: none -> 15.6 us  [per_device(): parts = lax.all_to_all(both, 'chip', 0, 0, tiled=True)]
    all_to_all x1 -> x0, waiting for transfers between devices: 7.7 us -> none  [per_device(): parts = lax.all_to_all(both, 'chip', 0, 0, tiled=True)]
    all_to_all x1 -> x0, starting transfers between devices: 6.75 us -> none  [per_device(): parts = lax.all_to_all(both, 'chip', 0, 0, tiled=True)]
    pallas_call x1, Pallas kernels: 0.79 us -> 0.04 us  [per_device(): pl.pallas_call(add_kernel, out_shape=jax.ShapeDtypeStruct(own.shape, jnp....]
    ppermute x1, waiting for transfers between devices: 0.56 us -> 0.01 us  [per_device(): arrived = lax.ppermute(theirs, 'core', [(0, 1), (1, 0)])]
  transfers between devices with their start and end apart: 2 -> 1, of which waited for: 2 -> 0; matrix products, arithmetic and copies ran while one was open for 0% -> 0% of each run, Pallas kernels for 2% -> 2%
where the time goes in v4:
time: 54.8 us; the launch traced here: 54.6 us
  blocking collectives  42.5 us (78%)
  Pallas kernels  6.1 us (11%)
  starting transfers between devices  4 us (7%)
  between operations  1.98 us (4%)
    all_to_all x1, blocking collectives, per_device(): lax.all_to_all(partial, 'shard', 0, 0, tiled=True, axis_index_groups=[lis...  26.8 us
    all_to_all x1, blocking collectives, per_device(): parts = lax.all_to_all(both, 'chip', 0, 0, tiled=True)  15.6 us
    ppermute x1, starting transfers between devices, per_device(): arrived = lax.ppermute(theirs, 'core', [(0, 1), (1, 0)])  4 us
    pallas_call x1, Pallas kernels, per_device(): pl.pallas_call(square_kernel, out_shape=(pltpu.VMEM(updates.shape, jnp.bf...  3.52 us
    pallas_call x2, Pallas kernels, weighted(): pl.pallas_call(weight, out_shape=jax.ShapeDtypeStruct((chips, 8, SLAB), j...  1.52 us
  transfers between devices with their start and end apart: 1, of which 0 were waited for; matrix products, arithmetic and copies ran while one was open for 0% of the time, Pallas kernels for 2%

profile of v4, /device:TPU:1, one launch (start us, length us, event | category | flops | bytes accessed | tf_op | source)
XLA Modules:
  0.0 54.6 jit_solution(694938901125064761)
XLA Ops:
  0.6 3.5 %squares.1 = (bf16[12,12,14336]{2,1,0:T(8,128)(2,1)S(1)}, f32[16,1,128]{2,1,0:T(1,128)S(1)}, f32[12,448]{1,0:T(8,128)S(1)}, s32[1,128]{1,0:T(1,128)S(1)}, f32[1,...) custom-call(f32[12]{0:T(128)} %log_hbm.1, s32[384]{0:T(512)} %cohort_hbm.1, s32[8]{0:T(128)} %seeds_hbm.1, ...), custom_call_target="tpu_custom_call" | custom-call | tf_op jit(solution)/shard_map/squares/pallas_call | solution.py:185
  4.2 26.8 %all_to_all.10.refs_2_ = f32[16,1,128]{2,1,0:T(1,128)S(1)} all-to-all(f32[16,1,128]{2,1,0:T(1,128)S(1)} %get-tuple-element.20), channel_id=1, replica_groups={{0,1,2,3,4,5,6,7,8,9,10,11,12,13,14,15},{16,17,18,19,20,21,22,23,24,25,..., dimensions={0} | all-to-all | bytes 16384 | tf_op jit(solution)/shard_map/all_to_all | solution.py:214
  31.0 0.8 %weighted_theirs.1 = f32[16,8,768]{2,1,0:T(8,128)S(1)} custom-call(f32[1,128]{1,0:T(1,128)S(1)} %get-tuple-element.17.refs_0_, f32[12,128]{1,0:T(8,128)S(1)} %get-tuple-element.18.refs_1_, f32[16,1,128]{2,1,0:T(1,128)S(1)} %all_to_all.10.refs_2_, bf16[12,12,14336]{2,1,0:T(8,128)(2,1)S(1)} %get-tuple-element.21.refs_3_), custom_call_target="tpu_custom_call" | custom-call | flops 4128768 | bytes 2064384 | tf_op jit(solution)/shard_map/weighted_theirs/pallas_call | solution.py:237
  31.8 4.0 %collective-permute-start = (f32[16,8,768]{2,1,0:T(8,128)S(1)}, f32[16,8,768]{2,1,0:T(8,128)S(1)}, u32[]{:S(2)}, u32[]{:S(2)}) collective-permute-start(f32[16,8,768]{2,1,0:T(8,128)S(1)} %weighted_theirs.1), channel_id=1, source_target_pairs={{0,16},{16,0},{1,17},{17,1},{2,18},{18,2},{3,19},{19,3},{4,20},{20... | collective-permute-start | bytes 1179656 | tf_op jit(solution)/shard_map/ppermute | solution.py:250
  37.1 0.2 base.1.refs_1_
  37.3 0.8 %weighted_own.1.one_ref = f32[16,8,768]{2,1,0:T(8,128)S(1)} custom-call(f32[1,128]{1,0:T(1,128)S(1)} %get-tuple-element.17.refs_0_, f32[12,128]{1,0:T(8,128)S(1)} %get-tuple-element.18.refs_1_, f32[16,1,128]{2,1,0:T(1,128)S(1)} %all_to_all.10.refs_2_, bf16[12,12,14336]{2,1,0:T(8,128)(2,1)S(1)} %get-tuple-element.21.refs_3_), custom_call_target="tpu_custom_call" | custom-call | flops 4128768 | bytes 2064384 | tf_op jit(solution)/shard_map/weighted_own/pallas_call | solution.py:237
  38.1 0.0 collective-permute-done.other_ref
  38.1 15.6 %all_to_all.11.refs_2_ = f32[16,8,768]{2,1,0:T(8,128)S(1)} all-to-all(f32[16,8,768]{2,1,0:T(8,128)S(1)} %add_cores.1), channel_id=1, replica_groups=mesh['chip'=16,'core'=2,'shard'=16] {'chip'}, dimensions={0} | all-to-all | bytes 786432 | tf_op jit(solution)/shard_map/all_to_all | solution.py:262
  53.8 0.8 %finish.1 = (f32[12,448]{1,0:T(8,128)}, f32[1,12]{1,0:T(1,128)}) custom-call(f32[1,128]{1,0:T(1,128)S(1)} %get-tuple-element.16.refs_3_.refs_0_, f32[12,448]{1,0:T(8,128)S(1)} %base.1.refs_1_, f32[16,8,768]{2,1,0:T(8,128)S(1)} %all_to_all.11.refs_2_), custom_call_target="tpu_custom_call" | custom-call | tf_op jit(solution)/shard_map/finish/pallas_call | solution.py:267
  (1 shorter events, 0.0 us)
Async XLA Ops:
  31.8 6.3 %collective-permute-start = (f32[16,8,768]{2,1,0:T(8,128)S(1)}, f32[16,8,768]{2,1,0:T(8,128)S(1)}, u32[]{:S(2)}, u32[]{:S(2)}) collective-permute-start(f32[16,8,768]{2,1,0:T(8,128)S(1)} %weighted_theirs.1), channel_id=1, source_target_pairs={{0,16},{16,0},{1,17},{17,1},{2,18},{18,2},{3,19},{19,3},{4,20},{20... | collective-permute-start | bytes 1179656 | tf_op jit(solution)/shard_map/ppermute | solution.py:250

commit v5 on v4

--- a/solution.py
+++ b/solution.py
@@ -47,14 +47,33 @@
                   log_s, cohort_s, seeds_s, sums_v, small_sems, sems):
     local_clients, row_count, width = held_ref.shape
     cohort_count = log_s.shape[0]
+    def arrival(c):
+        return pltpu.make_async_copy(updates_hbm.at[c], held_ref.at[c], sems.at[c])
+
+    early = 2
+    for c in range(early):
+        arrival(c).start()
     small = []
     for k, (source, target) in enumerate((
         (log_hbm, log_s), (cohort_hbm, cohort_s), (seeds_hbm, seeds_s), (momentum_hbm, momentum_ref),
     )):
         small.append(pltpu.make_async_copy(source, target, small_sems.at[k]))
         small[-1].start()
-    for c in range(local_clients):
-        pltpu.make_async_copy(updates_hbm.at[c], held_ref.at[c], sems.at[c]).start()
+    for c in range(early, local_clients):
+        arrival(c).start()
+
+    step = 2 * PAIR
+
+    def add_client(c, carry):
+        arrival(c).wait()
+        acc = jnp.zeros((row_count, step), jnp.float32)
+        for at in range(0, width, step):
+            block = held_ref[c, :, at : at + step].astype(jnp.float32)
+            acc = acc + block * block
+        sums_v[c] = fold(acc)
+        return carry
+
+    lax.fori_loop(0, early, add_client, 0)
     for copy in small:
         copy.wait()
 
@@ -75,18 +94,7 @@
         member_ref[c : c + 1, :] = jnp.where((lanes & (HALF - 1)) == cohort, 1.0, 0.0)
     limit_ref[...] = jnp.exp(own_logs)
 
-    step = 2 * PAIR
-
-    def add_client(c, carry):
-        pltpu.make_async_copy(updates_hbm.at[c], held_ref.at[c], sems.at[c]).wait()
-        acc = jnp.zeros((row_count, step), jnp.float32)
-        for at in range(0, width, step):
-            block = held_ref[c, :, at : at + step].astype(jnp.float32)
-            acc = acc + block * block
-        sums_v[c] = fold(acc)
-        return carry
-
-    lax.fori_loop(0, local_clients, add_client, 0)
+    lax.fori_loop(early, local_clients, add_client, 0)
     column = jnp.sum(jnp.sum(sums_v[...], axis=1), axis=1, keepdims=True)
     row = jnp.sum(jnp.where(diagonal(local_clients), column, 0.0), axis=0, keepdims=True)
     partial_ref[...] = jnp.broadcast_to(row[None], partial_ref.shape)
@@ -210,10 +218,7 @@
         for x in (log_thresholds, cohort_of, seeds, momentum, updates)
     ))
 
-    partial, round_index, coef_index = lax.optimization_barrier((partial, round_index, coef_index))
-    squares = lax.all_to_all(
-        partial, "shard", 0, 0, tiled=True, axis_index_groups=[list(range(shards))]
-    )
+    squares = lax.all_to_all(partial, "shard", 0, 0, tiled=True)
 
     def base_of(*refs):
         base_kernel(width, total_clients, seeds.shape[0], *refs)
@@ -247,18 +252,18 @@
         )(limit, member, squares, held)
 
     theirs = weighted(1)
+    theirs, round_index, coef_index = lax.optimization_barrier((theirs, round_index, coef_index))
     arrived = lax.ppermute(theirs, "core", [(0, 1), (1, 0)])
     own = weighted(0)
 
     both = pl.pallas_call(
         add_kernel,
-        out_shape=jax.ShapeDtypeStruct(own.shape, jnp.float32),
+        out_shape=pltpu.VMEM(own.shape, jnp.float32),
         in_specs=[vmem] * 2,
         out_specs=vmem,
         compiler_params=params,
         name="add_cores",
     )(own, arrived)
-    both, base = lax.optimization_barrier((both, base))
     parts = lax.all_to_all(both, "chip", 0, 0, tiled=True)
 
     def finish(*refs):

time: 54.8 us -> 54.8 us (level)
  blocking collectives: 42.5 us -> 26.8 us
  waiting for transfers between devices: 0.01 us -> 8.26 us
  starting transfers between devices: 4 us -> 10.8 us
  Pallas kernels: 6.1 us -> 6.68 us
    all_to_all x2 -> x1, blocking collectives: 42.5 us -> 26.8 us  [per_device(): squares = lax.all_to_all(partial, 'shard', 0, 0, tiled=True)]
    all_to_all x0 -> x1, waiting for transfers between devices: none -> 7.7 us  [per_device(): parts = lax.all_to_all(both, 'chip', 0, 0, tiled=True)]
    all_to_all x0 -> x1, starting transfers between devices: none -> 6.75 us  [per_device(): parts = lax.all_to_all(both, 'chip', 0, 0, tiled=True)]
    pallas_call x1, Pallas kernels: 0.04 us -> 0.79 us  [per_device(): pl.pallas_call(add_kernel, out_shape=pltpu.VMEM(own.shape, jnp.float32),...]
    ppermute x1, waiting for transfers between devices: 0.01 us -> 0.56 us  [per_device(): arrived = lax.ppermute(theirs, 'core', [(0, 1), (1, 0)])]
  transfers between devices with their start and end apart: 1 -> 2, of which waited for: 0 -> 2; matrix products, arithmetic and copies ran while one was open for 0% -> 0% of each run, Pallas kernels for 2% -> 2%
where the time goes in v5:
time: 54.8 us; the launch traced here: 54.5 us
  blocking collectives  26.8 us (49%)
  starting transfers between devices  10.8 us (20%)
  waiting for transfers between devices  8.26 us (15%)
  Pallas kernels  6.68 us (12%)
  between operations  1.97 us (4%)
    all_to_all x1, blocking collectives, per_device(): squares = lax.all_to_all(partial, 'shard', 0, 0, tiled=True)  26.8 us
    all_to_all x1, waiting for transfers between devices, per_device(): parts = lax.all_to_all(both, 'chip', 0, 0, tiled=True)  7.7 us
    all_to_all x1, starting transfers between devices, per_device(): parts = lax.all_to_all(both, 'chip', 0, 0, tiled=True)  6.75 us
    ppermute x1, starting transfers between devices, per_device(): arrived = lax.ppermute(theirs, 'core', [(0, 1), (1, 0)])  4 us
    pallas_call x1, Pallas kernels, per_device(): pl.pallas_call(square_kernel, out_shape=(pltpu.VMEM(updates.shape, jnp.bf...  3.35 us
    pallas_call x2, Pallas kernels, weighted(): pl.pallas_call(weight, out_shape=jax.ShapeDtypeStruct((chips, 8, SLAB), j...  1.52 us
  transfers between devices with their start and end apart: 2, of which 2 were waited for; matrix products, arithmetic and copies ran while one was open for 0% of the time, Pallas kernels for 2%

profile of v5, /device:TPU:1, one launch (start us, length us, event | category | flops | bytes accessed | tf_op | source)
XLA Modules:
  0.0 54.5 jit_solution(14798485516457153132)
XLA Ops:
  0.6 3.4 %squares.1 = (bf16[12,12,14336]{2,1,0:T(8,128)(2,1)S(1)}, f32[16,1,128]{2,1,0:T(1,128)S(1)}, f32[12,448]{1,0:T(8,128)S(1)}, s32[1,128]{1,0:T(1,128)S(1)}, f32[1,...) custom-call(f32[12]{0:T(128)} %log_hbm.1, s32[384]{0:T(512)} %cohort_hbm.1, s32[8]{0:T(128)} %seeds_hbm.1, ...), custom_call_target="tpu_custom_call" | custom-call | tf_op jit(solution)/shard_map/squares/pallas_call | solution.py:193
  4.0 26.8 %all_to_all.10.refs_2_ = f32[16,1,128]{2,1,0:T(1,128)S(1)} all-to-all(f32[16,1,128]{2,1,0:T(1,128)S(1)} %get-tuple-element.17), channel_id=1, replica_groups=mesh['chip'=16,'core'=2,'shard'=16] {'shard'}, dimensions={0} | all-to-all | bytes 16384 | tf_op jit(solution)/shard_map/all_to_all | solution.py:221
  30.8 0.8 %weighted_theirs.1 = f32[16,8,768]{2,1,0:T(8,128)S(1)} custom-call(f32[1,128]{1,0:T(1,128)S(1)} %get-tuple-element.15.refs_0_, f32[12,128]{1,0:T(8,128)S(1)} %get-tuple-element.16.refs_1_, f32[16,1,128]{2,1,0:T(1,128)S(1)} %all_to_all.10.refs_2_, bf16[12,12,14336]{2,1,0:T(8,128)(2,1)S(1)} %get-tuple-element.18.refs_3_), custom_call_target="tpu_custom_call" | custom-call | flops 4128768 | bytes 2064384 | tf_op jit(solution)/shard_map/weighted_theirs/pallas_call | solution.py:242
  31.6 4.0 %collective-permute-start = (f32[16,8,768]{2,1,0:T(8,128)S(1)}, f32[16,8,768]{2,1,0:T(8,128)S(1)}, u32[]{:S(2)}, u32[]{:S(2)}) collective-permute-start(f32[16,8,768]{2,1,0:T(8,128)S(1)} %weighted_theirs.1), channel_id=1, source_target_pairs={{0,16},{16,0},{1,17},{17,1},{2,18},{18,2},{3,19},{19,3},{4,20},{20... | collective-permute-start | bytes 1179656 | tf_op jit(solution)/shard_map/ppermute | solution.py:256
  35.6 0.8 %weighted_own.1.one_ref = f32[16,8,768]{2,1,0:T(8,128)S(1)} custom-call(f32[1,128]{1,0:T(1,128)S(1)} %get-tuple-element.15.refs_0_, f32[12,128]{1,0:T(8,128)S(1)} %get-tuple-element.16.refs_1_, f32[16,1,128]{2,1,0:T(1,128)S(1)} %all_to_all.10.refs_2_, bf16[12,12,14336]{2,1,0:T(8,128)(2,1)S(1)} %get-tuple-element.18.refs_3_), custom_call_target="tpu_custom_call" | custom-call | flops 4128768 | bytes 2064384 | tf_op jit(solution)/shard_map/weighted_own/pallas_call | solution.py:242
  36.4 0.6 %collective-permute-done.other_ref = f32[16,8,768]{2,1,0:T(8,128)S(1)} collective-permute-done((f32[16,8,768]{2,1,0:T(8,128)S(1)}, f32[16,8,768]{2,1,0:T(8,128)S(1)}, u32[]{:S(2)}, u32[]{:S(2)}) %collective-permute-start) | collective-permute-done | bytes 393248 | tf_op jit(solution)/shard_map/ppermute | solution.py:256
  36.9 0.8 %add_cores.1 = f32[16,8,768]{2,1,0:T(8,128)} custom-call(f32[16,8,768]{2,1,0:T(8,128)S(1)} %weighted_own.1.one_ref, f32[16,8,768]{2,1,0:T(8,128)S(1)} %collective-permute-done.other_ref), custom_call_target="tpu_custom_call" | custom-call | tf_op jit(solution)/shard_map/add_cores/pallas_call | solution.py:259
  37.7 6.8 %all-to-all-start.1 = ((f32[16,8,768]{2,1,0:T(8,128)}), f32[16,8,768]{2,1,0:T(8,128)S(1)}, u32[]{:S(2)}, u32[]{:S(2)}) async-start(f32[16,8,768]{2,1,0:T(8,128)} %add_cores.1), calls=%async_computation.1 | async-start | bytes 786432 | tf_op jit(solution)/shard_map/all_to_all | solution.py:267
  45.8 0.2 base.1.refs_1_
  46.0 7.7 %all-to-all-done.1.refs_2_ = f32[16,8,768]{2,1,0:T(8,128)S(1)} async-done(((f32[16,8,768]{2,1,0:T(8,128)}), f32[16,8,768]{2,1,0:T(8,128)S(1)}, u32[]{:S(2)}, u32[]{:S(2)}) %all-to-all-start.1) | async-done | bytes 393248 | tf_op jit(solution)/shard_map/all_to_all | solution.py:267
  53.7 0.8 %finish.1 = (f32[12,448]{1,0:T(8,128)}, f32[1,12]{1,0:T(1,128)}) custom-call(f32[1,128]{1,0:T(1,128)S(1)} %get-tuple-element.12.refs_3_.refs_0_, f32[12,448]{1,0:T(8,128)S(1)} %base.1.refs_1_, f32[16,8,768]{2,1,0:T(8,128)S(1)} %all-to-all-done.1.refs_2_), custom_call_target="tpu_custom_call" | custom-call | tf_op jit(solution)/shard_map/finish/pallas_call | solution.py:272
Async XLA Ops:
  31.6 5.3 %collective-permute-start = (f32[16,8,768]{2,1,0:T(8,128)S(1)}, f32[16,8,768]{2,1,0:T(8,128)S(1)}, u32[]{:S(2)}, u32[]{:S(2)}) collective-permute-start(f32[16,8,768]{2,1,0:T(8,128)S(1)} %weighted_theirs.1), channel_id=1, source_target_pairs={{0,16},{16,0},{1,17},{17,1},{2,18},{18,2},{3,19},{19,3},{4,20},{20... | collective-permute-start | bytes 1179656 | tf_op jit(solution)/shard_map/ppermute | solution.py:256
  37.7 16.0 %all-to-all-start.1 = ((f32[16,8,768]{2,1,0:T(8,128)}), f32[16,8,768]{2,1,0:T(8,128)S(1)}, u32[]{:S(2)}, u32[]{:S(2)}) async-start(f32[16,8,768]{2,1,0:T(8,128)} %add_cores.1), calls=%async_computation.1 | async-start | bytes 786432 | tf_op jit(solution)/shard_map/all_to_all | solution.py:267

commit v6 on v5

--- a/solution.py
+++ b/solution.py
@@ -100,7 +100,7 @@
     partial_ref[...] = jnp.broadcast_to(row[None], partial_ref.shape)
 
 
-def weight_kernel(other, limit_ref, member_ref, squares_ref, held_ref, slab_ref):
+def weight_kernel(other, limit_ref, member_ref, squares_ref, held_ref, _, slab_ref):
     local_clients, row_count, width = held_ref.shape
     odd = (lax.axis_index("core") + other) % 2
     norms = jnp.sqrt(jnp.sum(squares_ref[...], axis=0))
@@ -136,7 +136,7 @@
     lax.fori_loop(0, width // PAIR, pair, 0, unroll=4)
 
 
-def base_kernel(width, total_clients, band, round_s, coef_s, seeds_ref, log_ref, momentum_ref, base_ref):
+def base_kernel(width, total_clients, band, round_s, coef_s, seeds_ref, log_ref, momentum_ref, _, base_ref):
     rows, cols = momentum_ref.shape
     first_row = lax.axis_index("shard") * rows
     first_col = (2 * lax.axis_index("chip") + lax.axis_index("core")) * cols
@@ -187,6 +187,7 @@
     vmem = pl.BlockSpec(memory_space=pltpu.VMEM)
     hbm = pl.BlockSpec(memory_space=pltpu.HBM)
     smem = pl.BlockSpec(memory_space=pltpu.SMEM)
+    anywhere = pl.BlockSpec(memory_space=pl.ANY)
     params = pltpu.CompilerParams(vmem_limit_bytes=24 * MIB)
     row = jax.ShapeDtypeStruct((1, LANES), jnp.float32)
 
@@ -226,14 +227,14 @@
     base = pl.pallas_call(
         base_of,
         out_shape=jax.ShapeDtypeStruct((rows, cols), jnp.float32),
-        in_specs=[smem] * 2 + [vmem] * 3,
+        in_specs=[smem] * 2 + [vmem] * 3 + [anywhere],
         out_specs=vmem,
         compiler_params=params,
         cost_estimate=pl.CostEstimate(
             flops=200 * momentum.size, bytes_accessed=8 * momentum.size, transcendentals=0
         ),
         name="base",
-    )(round_index, coef_index, seed_row, log_row, momentum_v)
+    )(round_index, coef_index, seed_row, log_row, momentum_v, partial)
 
     def weighted(other):
         def weight(*refs):
@@ -242,23 +243,22 @@
         return pl.pallas_call(
             weight,
             out_shape=jax.ShapeDtypeStruct((chips, 8, SLAB), jnp.float32),
-            in_specs=[vmem] * 4,
+            in_specs=[vmem] * 4 + [anywhere],
             out_specs=vmem,
             compiler_params=params,
             cost_estimate=pl.CostEstimate(
                 flops=2 * updates.size, bytes_accessed=updates.size, transcendentals=0
             ),
             name="weighted_theirs" if other else "weighted_own",
-        )(limit, member, squares, held)
+        )(limit, member, squares, held, base)
 
     theirs = weighted(1)
-    theirs, round_index, coef_index = lax.optimization_barrier((theirs, round_index, coef_index))
     arrived = lax.ppermute(theirs, "core", [(0, 1), (1, 0)])
     own = weighted(0)
 
     both = pl.pallas_call(
         add_kernel,
-        out_shape=pltpu.VMEM(own.shape, jnp.float32),
+        out_shape=jax.ShapeDtypeStruct(own.shape, jnp.float32),
         in_specs=[vmem] * 2,
         out_specs=vmem,
         compiler_params=params,

time: 54.8 us -> 59.5 us (1.086)
  blocking collectives: 26.8 us -> 15.8 us
  starting transfers between devices: 10.8 us -> 19.7 us
  local copies, waits for them, and re-layouts: 0 us -> 4.96 us
  waiting for transfers between devices: 8.26 us -> 10.2 us
    all_to_all x1, blocking collectives: 26.8 us -> 15.8 us  [per_device(): parts = lax.all_to_all(both, 'chip', 0, 0, tiled=True)]
    all_to_all x1, starting transfers between devices: 6.75 us -> 15.7 us  [per_device(): squares = lax.all_to_all(partial, 'shard', 0, 0, tiled=True)]
    unnamed x0 -> x4, local copies, waits for them, and re-layouts: none -> 4.96 us
    all_to_all x1, waiting for transfers between devices: 7.7 us -> 9.69 us  [per_device(): squares = lax.all_to_all(partial, 'shard', 0, 0, tiled=True)]
    pallas_call x1, Pallas kernels: 0.79 us -> 0.04 us  [per_device(): pl.pallas_call(add_kernel, out_shape=jax.ShapeDtypeStruct(own.shape, jnp....]
    pallas_call x1, Pallas kernels: 3.35 us -> 3.95 us  [per_device(): pl.pallas_call(square_kernel, out_shape=(pltpu.VMEM(updates.shape, jnp.bf...]
where the time goes in v6:
time: 59.5 us; the launch traced here: 59.3 us
  starting transfers between devices  19.7 us (33%)
  blocking collectives  15.8 us (27%)
  waiting for transfers between devices  10.2 us (17%)
  Pallas kernels  6.54 us (11%)
  local copies, waits for them, and re-layouts  4.96 us (8%)
  between operations  1.99 us (3%)
    all_to_all x1, blocking collectives, per_device(): parts = lax.all_to_all(both, 'chip', 0, 0, tiled=True)  15.8 us
    all_to_all x1, starting transfers between devices, per_device(): squares = lax.all_to_all(partial, 'shard', 0, 0, tiled=True)  15.7 us
    all_to_all x1, waiting for transfers between devices, per_device(): squares = lax.all_to_all(partial, 'shard', 0, 0, tiled=True)  9.69 us
    unnamed x4, local copies, waits for them, and re-layouts  4.96 us
    ppermute x1, starting transfers between devices, per_device(): arrived = lax.ppermute(theirs, 'core', [(0, 1), (1, 0)])  4 us
    pallas_call x1, Pallas kernels, per_device(): pl.pallas_call(square_kernel, out_shape=(pltpu.VMEM(updates.shape, jnp.bf...  3.95 us
    pallas_call x2, Pallas kernels, weighted(): pl.pallas_call(weight, out_shape=jax.ShapeDtypeStruct((chips, 8, SLAB), j...  1.52 us
  transfers between devices with their start and end apart: 2, of which 2 were waited for; matrix products, arithmetic and copies ran while one was open for 0% of the time, Pallas kernels for 2%

profile of v6, /device:TPU:1, one launch (start us, length us, event | category | flops | bytes accessed | tf_op | source)
XLA Modules:
  0.0 59.3 jit_solution(10877761286630678082)
XLA Ops:
  0.6 3.9 %squares.1 = (bf16[12,12,14336]{2,1,0:T(8,128)(2,1)S(1)}, f32[16,1,128]{2,1,0:T(1,128)}, f32[12,448]{1,0:T(8,128)S(1)}, s32[1,128]{1,0:T(1,128)S(1)}, f32[1,128]...) custom-call(f32[12]{0:T(128)} %log_hbm.1, s32[384]{0:T(512)} %cohort_hbm.1, s32[8]{0:T(128)} %seeds_hbm.1, ...), custom_call_target="tpu_custom_call" | custom-call | tf_op jit(solution)/shard_map/squares/pallas_call | solution.py:194
  4.6 0.0 copy-start
  4.6 2.4 %copy-done = bf16[12,12,14336]{2,1,0:T(8,128)(2,1)} copy-done((bf16[12,12,14336]{2,1,0:T(8,128)(2,1)}, bf16[12,12,14336]{2,1,0:T(8,128)(2,1)S(1)}, u32[]{:S(2)}) %copy-start) | copy-done | bytes 4128792
  7.0 15.7 %all-to-all-start = ((f32[16,1,128]{2,1,0:T(1,128)}), f32[16,1,128]{2,1,0:T(1,128)S(1)}, u32[]{:S(2)}, u32[]{:S(2)}) async-start(f32[16,1,128]{2,1,0:T(1,128)} %get-tuple-element.14.refs_5_), calls=%async_computation | async-start | bytes 16384 | tf_op jit(solution)/shard_map/all_to_all | solution.py:222
  24.0 0.2 base.1.refs_4_.refs_1_
  24.3 9.7 %all-to-all-done.refs_2_ = f32[16,1,128]{2,1,0:T(1,128)S(1)} async-done(((f32[16,1,128]{2,1,0:T(1,128)}), f32[16,1,128]{2,1,0:T(1,128)S(1)}, u32[]{:S(2)}, u32[]{:S(2)}) %all-to-all-start) | async-done | bytes 8224 | tf_op jit(solution)/shard_map/all_to_all | solution.py:222
  34.0 0.0 copy-start.1
  34.0 2.6 %copy-done.1 = bf16[12,12,14336]{2,1,0:T(8,128)(2,1)S(1)} copy-done((bf16[12,12,14336]{2,1,0:T(8,128)(2,1)S(1)}, bf16[12,12,14336]{2,1,0:T(8,128)(2,1)}, u32[]{:S(2)}) %copy-start.1) | copy-done | bytes 4128792
  36.5 0.8 %weighted_theirs.1 = f32[16,8,768]{2,1,0:T(8,128)S(1)} custom-call(f32[1,128]{1,0:T(1,128)S(1)} %get-tuple-element.15.refs_0_, f32[12,128]{1,0:T(8,128)S(1)} %get-tuple-element.16.refs_1_, f32[16,1,128]{2,1,0:T(1,128)S(1)} %all-to-all-done.refs_2_, bf16[12,12,14336]{2,1,0:T(8,128)(2,1)S(1)} %copy-done.1, f32[12,448]{1,0:T(8,128)S(1)} %base.1.refs_4_.refs_1_), custom_call_target="tpu_custom_call" | custom-call | flops 4128768 | bytes 2064384 | tf_op jit(solution)/shard_map/weighted_theirs/pallas_call | solution.py:243
  37.3 4.0 %collective-permute-start = (f32[16,8,768]{2,1,0:T(8,128)S(1)}, f32[16,8,768]{2,1,0:T(8,128)S(1)}, u32[]{:S(2)}, u32[]{:S(2)}) collective-permute-start(f32[16,8,768]{2,1,0:T(8,128)S(1)} %weighted_theirs.1), channel_id=1, source_target_pairs={{0,16},{16,0},{1,17},{17,1},{2,18},{18,2},{3,19},{19,3},{4,20},{20... | collective-permute-start | bytes 1179656 | tf_op jit(solution)/shard_map/ppermute | solution.py:256
  41.3 0.8 %weighted_own.1.one_ref = f32[16,8,768]{2,1,0:T(8,128)S(1)} custom-call(f32[1,128]{1,0:T(1,128)S(1)} %get-tuple-element.15.refs_0_, f32[12,128]{1,0:T(8,128)S(1)} %get-tuple-element.16.refs_1_, f32[16,1,128]{2,1,0:T(1,128)S(1)} %all-to-all-done.refs_2_, bf16[12,12,14336]{2,1,0:T(8,128)(2,1)S(1)} %copy-done.1, f32[12,448]{1,0:T(8,128)S(1)} %base.1.refs_4_.refs_1_), custom_call_target="tpu_custom_call" | custom-call | flops 4128768 | bytes 2064384 | tf_op jit(solution)/shard_map/weighted_own/pallas_call | solution.py:243
  42.1 0.6 collective-permute-done.other_ref
  42.7 15.8 %all_to_all.10.refs_2_ = f32[16,8,768]{2,1,0:T(8,128)S(1)} all-to-all(f32[16,8,768]{2,1,0:T(8,128)S(1)} %add_cores.1), channel_id=1, replica_groups=mesh['chip'=16,'core'=2,'shard'=16] {'chip'}, dimensions={0} | all-to-all | bytes 786432 | tf_op jit(solution)/shard_map/all_to_all | solution.py:267
  58.5 0.8 %finish.1 = (f32[12,448]{1,0:T(8,128)}, f32[1,12]{1,0:T(1,128)}) custom-call(f32[1,128]{1,0:T(1,128)S(1)} %get-tuple-element.11.refs_3_.refs_0_, f32[12,448]{1,0:T(8,128)S(1)} %base.1.refs_4_.refs_1_, f32[16,8,768]{2,1,0:T(8,128)S(1)} %all_to_all.10.refs_2_), custom_call_target="tpu_custom_call" | custom-call | tf_op jit(solution)/shard_map/finish/pallas_call | solution.py:272
  (1 shorter events, 0.0 us)
Async XLA Ops:
  4.6 2.4 %copy-start = (bf16[12,12,14336]{2,1,0:T(8,128)(2,1)}, bf16[12,12,14336]{2,1,0:T(8,128)(2,1)S(1)}, u32[]{:S(2)}) copy-start(bf16[12,12,14336]{2,1,0:T(8,128)(2,1)S(1)} %get-tuple-element.17.refs_3_) | copy-start | bytes 12386308
  7.0 27.0 %all-to-all-start = ((f32[16,1,128]{2,1,0:T(1,128)}), f32[16,1,128]{2,1,0:T(1,128)S(1)}, u32[]{:S(2)}, u32[]{:S(2)}) async-start(f32[16,1,128]{2,1,0:T(1,128)} %get-tuple-element.14.refs_5_), calls=%async_computation | async-start | bytes 16384 | tf_op jit(solution)/shard_map/all_to_all | solution.py:222
  34.0 2.6 %copy-start.1 = (bf16[12,12,14336]{2,1,0:T(8,128)(2,1)S(1)}, bf16[12,12,14336]{2,1,0:T(8,128)(2,1)}, u32[]{:S(2)}) copy-start(bf16[12,12,14336]{2,1,0:T(8,128)(2,1)} %copy-done) | copy-start | bytes 12386308
  37.3 5.3 %collective-permute-start = (f32[16,8,768]{2,1,0:T(8,128)S(1)}, f32[16,8,768]{2,1,0:T(8,128)S(1)}, u32[]{:S(2)}, u32[]{:S(2)}) collective-permute-start(f32[16,8,768]{2,1,0:T(8,128)S(1)} %weighted_theirs.1), channel_id=1, source_target_pairs={{0,16},{16,0},{1,17},{17,1},{2,18},{18,2},{3,19},{19,3},{4,20},{20... | collective-permute-start | bytes 1179656 | tf_op jit(solution)/shard_map/ppermute | solution.py:256

commit v7 on v5

--- a/solution.py
+++ b/solution.py
@@ -1,3 +1,5 @@
+import math
+
 import jax
 import jax.numpy as jnp
 from jax import lax
@@ -96,14 +98,13 @@
 
     lax.fori_loop(early, local_clients, add_client, 0)
     column = jnp.sum(jnp.sum(sums_v[...], axis=1), axis=1, keepdims=True)
-    row = jnp.sum(jnp.where(diagonal(local_clients), column, 0.0), axis=0, keepdims=True)
-    partial_ref[...] = jnp.broadcast_to(row[None], partial_ref.shape)
+    partial_ref[...] = jnp.sum(jnp.where(diagonal(local_clients), column, 0.0), axis=0, keepdims=True)
 
 
 def weight_kernel(other, limit_ref, member_ref, squares_ref, held_ref, slab_ref):
     local_clients, row_count, width = held_ref.shape
     odd = (lax.axis_index("core") + other) % 2
-    norms = jnp.sqrt(jnp.sum(squares_ref[...], axis=0))
+    norms = jnp.sqrt(squares_ref[...])
     limit = limit_ref[...]
     factor = limit / jnp.maximum(norms, limit)
     factors = [jnp.broadcast_to(factor[:, c : c + 1], (row_count, REACH)) for c in range(local_clients)]
@@ -194,7 +195,7 @@
         square_kernel,
         out_shape=(
             pltpu.VMEM(updates.shape, jnp.bfloat16),
-            jax.ShapeDtypeStruct((shards, 1, LANES), jnp.float32),
+            row,
             pltpu.VMEM((rows, cols), jnp.float32),
             jax.ShapeDtypeStruct((1, LANES), jnp.int32),
             row,
@@ -218,7 +219,11 @@
         for x in (log_thresholds, cohort_of, seeds, momentum, updates)
     ))
 
-    squares = lax.all_to_all(partial, "shard", 0, 0, tiled=True)
+    ring = math.isqrt(shards)
+    near = [[ring * i + j for j in range(ring)] for i in range(shards // ring)]
+    far = [[ring * i + j for i in range(shards // ring)] for j in range(ring)]
+    squares = lax.psum(partial, "shard", axis_index_groups=near)
+    squares = lax.psum(squares, "shard", axis_index_groups=far)
 
     def base_of(*refs):
         base_kernel(width, total_clients, seeds.shape[0], *refs)

time: 54.8 us -> 63.8 us (1.16)
  local copies, waits for them, and re-layouts: 0 us -> 4.93 us
  starting transfers between devices: 10.8 us -> 13 us
  blocking collectives: 26.8 us -> 28.6 us
    psum x0 -> x2, blocking collectives: none -> 28.6 us  [the longest x1 16.9 us: per_device(): squares = lax.psum(squares, 'shard', axis_index_groups=far)]
    all_to_all x1 -> x0, blocking collectives: 26.8 us -> none  [per_device(): squares = lax.all_to_all(partial, 'shard', 0, 0, tiled=True)]
    unnamed x0 -> x4, local copies, waits for them, and re-layouts: none -> 4.93 us
    ppermute x1, starting transfers between devices: 4 us -> 6.28 us  [per_device(): arrived = lax.ppermute(theirs, 'core', [(0, 1), (1, 0)])]
where the time goes in v7:
time: 63.8 us; the launch traced here: 63.5 us
  blocking collectives  28.6 us (45%)
  starting transfers between devices  13 us (20%)
  waiting for transfers between devices  8.27 us (13%)
  Pallas kernels  6.65 us (10%)
  local copies, waits for them, and re-layouts  4.93 us (8%)
  between operations  1.98 us (3%)
    psum x1, blocking collectives, per_device(): squares = lax.psum(squares, 'shard', axis_index_groups=far)  16.9 us
    psum x1, blocking collectives, per_device(): squares = lax.psum(partial, 'shard', axis_index_groups=near)  11.8 us
    all_to_all x1, waiting for transfers between devices, per_device(): parts = lax.all_to_all(both, 'chip', 0, 0, tiled=True)  7.7 us
    all_to_all x1, starting transfers between devices, per_device(): parts = lax.all_to_all(both, 'chip', 0, 0, tiled=True)  6.75 us
    ppermute x1, starting transfers between devices, per_device(): arrived = lax.ppermute(theirs, 'core', [(0, 1), (1, 0)])  6.28 us
    unnamed x4, local copies, waits for them, and re-layouts  4.93 us
    pallas_call x1, Pallas kernels, per_device(): pl.pallas_call(square_kernel, out_shape=(pltpu.VMEM(updates.shape, jnp.bf...  3.35 us
    pallas_call x2, Pallas kernels, weighted(): pl.pallas_call(weight, out_shape=jax.ShapeDtypeStruct((chips, 8, SLAB), j...  1.5 us
  transfers between devices with their start and end apart: 2, of which 2 were waited for; matrix products, arithmetic and copies ran while one was open for 0% of the time, Pallas kernels for 2%

profile of v7, /device:TPU:1, one launch (start us, length us, event | category | flops | bytes accessed | tf_op | source)
XLA Modules:
  0.0 63.5 jit_solution(12896742417408370092)
XLA Ops:
  0.6 3.3 %squares.1 = (bf16[12,12,14336]{2,1,0:T(8,128)(2,1)S(1)}, f32[1,128]{1,0:T(1,128)S(1)}, f32[12,448]{1,0:T(8,128)S(1)}, s32[1,128]{1,0:T(1,128)S(1)}, f32[1,128]{...) custom-call(f32[12]{0:T(128)} %log_hbm.1, s32[384]{0:T(512)} %cohort_hbm.1, s32[8]{0:T(128)} %seeds_hbm.1, ...), custom_call_target="tpu_custom_call" | custom-call | tf_op jit(solution)/shard_map/squares/pallas_call | solution.py:194
  4.0 0.0 copy-start
  4.0 2.4 %copy-done = bf16[12,12,14336]{2,1,0:T(8,128)(2,1)} copy-done((bf16[12,12,14336]{2,1,0:T(8,128)(2,1)}, bf16[12,12,14336]{2,1,0:T(8,128)(2,1)S(1)}, u32[]{:S(2)}) %copy-start) | copy-done | bytes 4128792
  6.4 11.8 %psum.14 = f32[1,128]{1,0:T(1,128)S(1)} all-reduce(f32[1,128]{1,0:T(1,128)S(1)} %get-tuple-element.17), channel_id=1, replica_groups={{0,1,2,3},{4,5,6,7},{8,9,10,11},{12,13,14,15},{16,17,18,19},{20,21,22,2..., use_global_device_ids=true, to_apply=%region_0.0 | all-reduce | flops 128 | bytes 1024 | tf_op jit(solution)/shard_map/psum | solution.py:225
  18.1 16.9 %psum.15.refs_2_ = f32[1,128]{1,0:T(1,128)S(1)} all-reduce(f32[1,128]{1,0:T(1,128)S(1)} %psum.14), channel_id=1, replica_groups={{0,4,8,12},{1,5,9,13},{2,6,10,14},{3,7,11,15},{16,20,24,28},{17,21,25,2..., use_global_device_ids=true, to_apply=%region_1.0 | all-reduce | flops 128 | bytes 1024 | tf_op jit(solution)/shard_map/psum | solution.py:226
  35.0 0.0 copy-start.1
  35.0 2.6 %copy-done.1 = bf16[12,12,14336]{2,1,0:T(8,128)(2,1)S(1)} copy-done((bf16[12,12,14336]{2,1,0:T(8,128)(2,1)S(1)}, bf16[12,12,14336]{2,1,0:T(8,128)(2,1)}, u32[]{:S(2)}) %copy-start.1) | copy-done | bytes 4128792
  37.6 0.7 %weighted_theirs.1 = f32[16,8,768]{2,1,0:T(8,128)S(1)} custom-call(f32[1,128]{1,0:T(1,128)S(1)} %get-tuple-element.15.refs_0_, f32[12,128]{1,0:T(8,128)S(1)} %get-tuple-element.16.refs_1_, f32[1,128]{1,0:T(1,128)S(1)} %psum.15.refs_2_, bf16[12,12,14336]{2,1,0:T(8,128)(2,1)S(1)} %copy-done.1), custom_call_target="tpu_custom_call" | custom-call | flops 4128768 | bytes 2064384 | tf_op jit(solution)/shard_map/weighted_theirs/pallas_call | solution.py:247
  38.3 6.3 %collective-permute-start = (f32[16,8,768]{2,1,0:T(8,128)S(1)}, f32[16,8,768]{2,1,0:T(8,128)S(1)}, u32[]{:S(2)}, u32[]{:S(2)}) collective-permute-start(f32[16,8,768]{2,1,0:T(8,128)S(1)} %weighted_theirs.1), channel_id=1, source_target_pairs={{0,16},{16,0},{1,17},{17,1},{2,18},{18,2},{3,19},{19,3},{4,20},{20... | collective-permute-start | bytes 1179656 | tf_op jit(solution)/shard_map/ppermute | solution.py:261
  44.6 0.8 %weighted_own.1.one_ref = f32[16,8,768]{2,1,0:T(8,128)S(1)} custom-call(f32[1,128]{1,0:T(1,128)S(1)} %get-tuple-element.15.refs_0_, f32[12,128]{1,0:T(8,128)S(1)} %get-tuple-element.16.refs_1_, f32[1,128]{1,0:T(1,128)S(1)} %psum.15.refs_2_, bf16[12,12,14336]{2,1,0:T(8,128)(2,1)S(1)} %copy-done.1), custom_call_target="tpu_custom_call" | custom-call | flops 4128768 | bytes 2064384 | tf_op jit(solution)/shard_map/weighted_own/pallas_call | solution.py:247
  45.4 0.6 collective-permute-done.other_ref
  45.9 0.8 %add_cores.1 = f32[16,8,768]{2,1,0:T(8,128)} custom-call(f32[16,8,768]{2,1,0:T(8,128)S(1)} %weighted_own.1.one_ref, f32[16,8,768]{2,1,0:T(8,128)S(1)} %collective-permute-done.other_ref), custom_call_target="tpu_custom_call" | custom-call | tf_op jit(solution)/shard_map/add_cores/pallas_call | solution.py:264
  46.7 6.8 %all-to-all-start = ((f32[16,8,768]{2,1,0:T(8,128)}), f32[16,8,768]{2,1,0:T(8,128)S(1)}, u32[]{:S(2)}, u32[]{:S(2)}) async-start(f32[16,8,768]{2,1,0:T(8,128)} %add_cores.1), calls=%async_computation | async-start | bytes 786432 | tf_op jit(solution)/shard_map/all_to_all | solution.py:272
  54.8 0.2 base.1.refs_1_
  55.0 7.7 %all-to-all-done.refs_2_ = f32[16,8,768]{2,1,0:T(8,128)S(1)} async-done(((f32[16,8,768]{2,1,0:T(8,128)}), f32[16,8,768]{2,1,0:T(8,128)S(1)}, u32[]{:S(2)}, u32[]{:S(2)}) %all-to-all-start) | async-done | bytes 393248 | tf_op jit(solution)/shard_map/all_to_all | solution.py:272
  62.7 0.8 %finish.1 = (f32[12,448]{1,0:T(8,128)}, f32[1,12]{1,0:T(1,128)}) custom-call(f32[1,128]{1,0:T(1,128)S(1)} %get-tuple-element.12.refs_3_.refs_0_, f32[12,448]{1,0:T(8,128)S(1)} %base.1.refs_1_, f32[16,8,768]{2,1,0:T(8,128)S(1)} %all-to-all-done.refs_2_), custom_call_target="tpu_custom_call" | custom-call | tf_op jit(solution)/shard_map/finish/pallas_call | solution.py:277
Async XLA Ops:
  4.0 2.4 %copy-start = (bf16[12,12,14336]{2,1,0:T(8,128)(2,1)}, bf16[12,12,14336]{2,1,0:T(8,128)(2,1)S(1)}, u32[]{:S(2)}) copy-start(bf16[12,12,14336]{2,1,0:T(8,128)(2,1)S(1)} %get-tuple-element.18.refs_3_) | copy-start | bytes 12386308
  35.0 2.6 %copy-start.1 = (bf16[12,12,14336]{2,1,0:T(8,128)(2,1)S(1)}, bf16[12,12,14336]{2,1,0:T(8,128)(2,1)}, u32[]{:S(2)}) copy-start(bf16[12,12,14336]{2,1,0:T(8,128)(2,1)} %copy-done) | copy-start | bytes 12386308
  38.3 7.6 %collective-permute-start = (f32[16,8,768]{2,1,0:T(8,128)S(1)}, f32[16,8,768]{2,1,0:T(8,128)S(1)}, u32[]{:S(2)}, u32[]{:S(2)}) collective-permute-start(f32[16,8,768]{2,1,0:T(8,128)S(1)} %weighted_theirs.1), channel_id=1, source_target_pairs={{0,16},{16,0},{1,17},{17,1},{2,18},{18,2},{3,19},{19,3},{4,20},{20... | collective-permute-start | bytes 1179656 | tf_op jit(solution)/shard_map/ppermute | solution.py:261
  46.7 16.0 %all-to-all-start = ((f32[16,8,768]{2,1,0:T(8,128)}), f32[16,8,768]{2,1,0:T(8,128)S(1)}, u32[]{:S(2)}, u32[]{:S(2)}) async-start(f32[16,8,768]{2,1,0:T(8,128)} %add_cores.1), calls=%async_computation | async-start | bytes 786432 | tf_op jit(solution)/shard_map/all_to_all | solution.py:272

commit v8 on v5

--- a/solution.py
+++ b/solution.py
@@ -50,7 +50,7 @@
     def arrival(c):
         return pltpu.make_async_copy(updates_hbm.at[c], held_ref.at[c], sems.at[c])
 
-    early = 2
+    early, ahead = 2, 6
     for c in range(early):
         arrival(c).start()
     small = []
@@ -59,21 +59,29 @@
     )):
         small.append(pltpu.make_async_copy(source, target, small_sems.at[k]))
         small[-1].start()
-    for c in range(early, local_clients):
+    for c in range(early, ahead):
         arrival(c).start()
 
     step = 2 * PAIR
 
-    def add_client(c, carry):
+    def add_client(c, follows):
         arrival(c).wait()
+        if follows:
+            arrival(c + ahead).start()
         acc = jnp.zeros((row_count, step), jnp.float32)
         for at in range(0, width, step):
             block = held_ref[c, :, at : at + step].astype(jnp.float32)
             acc = acc + block * block
-        sums_v[c] = fold(acc)
-        return carry
-
-    lax.fori_loop(0, early, add_client, 0)
+        sums_v[c] = jnp.sum(fold(acc), axis=0, keepdims=True)
+
+    def add_clients(first, last, follows):
+        def step(c, carry):
+            add_client(c, follows)
+            return carry
+
+        lax.fori_loop(first, last, step, 0)
+
+    add_clients(0, early, True)
     for copy in small:
         copy.wait()
 
@@ -94,8 +102,9 @@
         member_ref[c : c + 1, :] = jnp.where((lanes & (HALF - 1)) == cohort, 1.0, 0.0)
     limit_ref[...] = jnp.exp(own_logs)
 
-    lax.fori_loop(early, local_clients, add_client, 0)
-    column = jnp.sum(jnp.sum(sums_v[...], axis=1), axis=1, keepdims=True)
+    add_clients(early, local_clients - ahead, True)
+    add_clients(local_clients - ahead, local_clients, False)
+    column = jnp.sum(sums_v[...][:, 0, :], axis=1, keepdims=True)
     row = jnp.sum(jnp.where(diagonal(local_clients), column, 0.0), axis=0, keepdims=True)
     partial_ref[...] = jnp.broadcast_to(row[None], partial_ref.shape)
 
@@ -207,7 +216,7 @@
             pltpu.SMEM((cohort_count,), jnp.float32),
             pltpu.SMEM((total_clients,), jnp.int32),
             pltpu.SMEM(seeds.shape, jnp.int32),
-            pltpu.VMEM((local_clients, rows, LANES), jnp.float32),
+            pltpu.VMEM((local_clients, 1, LANES), jnp.float32),
             pltpu.SemaphoreType.DMA((4,)),
             pltpu.SemaphoreType.DMA((local_clients,)),
         ],
@@ -218,7 +227,10 @@
         for x in (log_thresholds, cohort_of, seeds, momentum, updates)
     ))
 
-    squares = lax.all_to_all(partial, "shard", 0, 0, tiled=True)
+    partial, round_index, coef_index = lax.optimization_barrier((partial, round_index, coef_index))
+    squares = lax.all_to_all(
+        partial, "shard", 0, 0, tiled=True, axis_index_groups=[list(range(shards))]
+    )
 
     def base_of(*refs):
         base_kernel(width, total_clients, seeds.shape[0], *refs)
@@ -252,18 +264,18 @@
         )(limit, member, squares, held)
 
     theirs = weighted(1)
-    theirs, round_index, coef_index = lax.optimization_barrier((theirs, round_index, coef_index))
     arrived = lax.ppermute(theirs, "core", [(0, 1), (1, 0)])
     own = weighted(0)
 
     both = pl.pallas_call(
         add_kernel,
-        out_shape=pltpu.VMEM(own.shape, jnp.float32),
+        out_shape=jax.ShapeDtypeStruct(own.shape, jnp.float32),
         in_specs=[vmem] * 2,
         out_specs=vmem,
         compiler_params=params,
         name="add_cores",
     )(own, arrived)
+    both, base = lax.optimization_barrier((both, base))
     parts = lax.all_to_all(both, "chip", 0, 0, tiled=True)
 
     def finish(*refs):

time: 54.8 us -> 54.7 us (level)
  blocking collectives: 26.8 us -> 42.5 us
  waiting for transfers between devices: 8.26 us -> 0.01 us
  starting transfers between devices: 10.8 us -> 4 us
  Pallas kernels: 6.68 us -> 5.94 us
    all_to_all x1 -> x2, blocking collectives: 26.8 us -> 42.5 us  [the longest x1 26.8 us: per_device(): lax.all_to_all(partial, 'shard', 0, 0, tiled=True, axis_index_groups=[lis...]
    all_to_all x1 -> x0, waiting for transfers between devices: 7.7 us -> none  [per_device(): parts = lax.all_to_all(both, 'chip', 0, 0, tiled=True)]
    all_to_all x1 -> x0, starting transfers between devices: 6.75 us -> none  [per_device(): parts = lax.all_to_all(both, 'chip', 0, 0, tiled=True)]
    pallas_call x1, Pallas kernels: 0.79 us -> 0.04 us  [per_device(): pl.pallas_call(add_kernel, out_shape=jax.ShapeDtypeStruct(own.shape, jnp....]
    ppermute x1, waiting for transfers between devices: 0.56 us -> 0.01 us  [per_device(): arrived = lax.ppermute(theirs, 'core', [(0, 1), (1, 0)])]
  transfers between devices with their start and end apart: 2 -> 1, of which waited for: 2 -> 0; matrix products, arithmetic and copies ran while one was open for 0% -> 0% of each run, Pallas kernels for 2% -> 2%
where the time goes in v8:
time: 54.7 us; the launch traced here: 54.4 us
  blocking collectives  42.5 us (78%)
  Pallas kernels  5.94 us (11%)
  starting transfers between devices  4 us (7%)
  between operations  1.98 us (4%)
    all_to_all x1, blocking collectives, per_device(): lax.all_to_all(partial, 'shard', 0, 0, tiled=True, axis_index_groups=[lis...  26.8 us
    all_to_all x1, blocking collectives, per_device(): parts = lax.all_to_all(both, 'chip', 0, 0, tiled=True)  15.6 us
    ppermute x1, starting transfers between devices, per_device(): arrived = lax.ppermute(theirs, 'core', [(0, 1), (1, 0)])  4 us
    pallas_call x1, Pallas kernels, per_device(): pl.pallas_call(square_kernel, out_shape=(pltpu.VMEM(updates.shape, jnp.bf...  3.35 us
    pallas_call x2, Pallas kernels, weighted(): pl.pallas_call(weight, out_shape=jax.ShapeDtypeStruct((chips, 8, SLAB), j...  1.52 us
  transfers between devices with their start and end apart: 1, of which 0 were waited for; matrix products, arithmetic and copies ran while one was open for 0% of the time, Pallas kernels for 2%

profile of v8, /device:TPU:1, one launch (start us, length us, event | category | flops | bytes accessed | tf_op | source)
XLA Modules:
  0.0 54.4 jit_solution(10462868528207822136)
XLA Ops:
  0.6 3.4 %squares.1 = (bf16[12,12,14336]{2,1,0:T(8,128)(2,1)S(1)}, f32[16,1,128]{2,1,0:T(1,128)S(1)}, f32[12,448]{1,0:T(8,128)S(1)}, s32[1,128]{1,0:T(1,128)S(1)}, f32[1,...) custom-call(f32[12]{0:T(128)} %log_hbm.1, s32[384]{0:T(512)} %cohort_hbm.1, s32[8]{0:T(128)} %seeds_hbm.1, ...), custom_call_target="tpu_custom_call" | custom-call | tf_op jit(solution)/shard_map/squares/pallas_call | solution.py:202
  4.0 26.8 %all_to_all.10.refs_2_ = f32[16,1,128]{2,1,0:T(1,128)S(1)} all-to-all(f32[16,1,128]{2,1,0:T(1,128)S(1)} %get-tuple-element.20), channel_id=1, replica_groups={{0,1,2,3,4,5,6,7,8,9,10,11,12,13,14,15},{16,17,18,19,20,21,22,23,24,25,..., dimensions={0} | all-to-all | bytes 16384 | tf_op jit(solution)/shard_map/all_to_all | solution.py:231
  30.8 0.8 %weighted_theirs.1 = f32[16,8,768]{2,1,0:T(8,128)S(1)} custom-call(f32[1,128]{1,0:T(1,128)S(1)} %get-tuple-element.17.refs_0_, f32[12,128]{1,0:T(8,128)S(1)} %get-tuple-element.18.refs_1_, f32[16,1,128]{2,1,0:T(1,128)S(1)} %all_to_all.10.refs_2_, bf16[12,12,14336]{2,1,0:T(8,128)(2,1)S(1)} %get-tuple-element.21.refs_3_), custom_call_target="tpu_custom_call" | custom-call | flops 4128768 | bytes 2064384 | tf_op jit(solution)/shard_map/weighted_theirs/pallas_call | solution.py:254
  31.6 4.0 %collective-permute-start = (f32[16,8,768]{2,1,0:T(8,128)S(1)}, f32[16,8,768]{2,1,0:T(8,128)S(1)}, u32[]{:S(2)}, u32[]{:S(2)}) collective-permute-start(f32[16,8,768]{2,1,0:T(8,128)S(1)} %weighted_theirs.1), channel_id=1, source_target_pairs={{0,16},{16,0},{1,17},{17,1},{2,18},{18,2},{3,19},{19,3},{4,20},{20... | collective-permute-start | bytes 1179656 | tf_op jit(solution)/shard_map/ppermute | solution.py:267
  36.9 0.2 base.1.refs_1_
  37.1 0.8 %weighted_own.1.one_ref = f32[16,8,768]{2,1,0:T(8,128)S(1)} custom-call(f32[1,128]{1,0:T(1,128)S(1)} %get-tuple-element.17.refs_0_, f32[12,128]{1,0:T(8,128)S(1)} %get-tuple-element.18.refs_1_, f32[16,1,128]{2,1,0:T(1,128)S(1)} %all_to_all.10.refs_2_, bf16[12,12,14336]{2,1,0:T(8,128)(2,1)S(1)} %get-tuple-element.21.refs_3_), custom_call_target="tpu_custom_call" | custom-call | flops 4128768 | bytes 2064384 | tf_op jit(solution)/shard_map/weighted_own/pallas_call | solution.py:254
  37.9 0.0 collective-permute-done.other_ref
  38.0 15.6 %all_to_all.11.refs_2_ = f32[16,8,768]{2,1,0:T(8,128)S(1)} all-to-all(f32[16,8,768]{2,1,0:T(8,128)S(1)} %add_cores.1), channel_id=1, replica_groups=mesh['chip'=16,'core'=2,'shard'=16] {'chip'}, dimensions={0} | all-to-all | bytes 786432 | tf_op jit(solution)/shard_map/all_to_all | solution.py:279
  53.6 0.8 %finish.1 = (f32[12,448]{1,0:T(8,128)}, f32[1,12]{1,0:T(1,128)}) custom-call(f32[1,128]{1,0:T(1,128)S(1)} %get-tuple-element.16.refs_3_.refs_0_, f32[12,448]{1,0:T(8,128)S(1)} %base.1.refs_1_, f32[16,8,768]{2,1,0:T(8,128)S(1)} %all_to_all.11.refs_2_), custom_call_target="tpu_custom_call" | custom-call | tf_op jit(solution)/shard_map/finish/pallas_call | solution.py:284
  (1 shorter events, 0.0 us)
Async XLA Ops:
  31.6 6.3 %collective-permute-start = (f32[16,8,768]{2,1,0:T(8,128)S(1)}, f32[16,8,768]{2,1,0:T(8,128)S(1)}, u32[]{:S(2)}, u32[]{:S(2)}) collective-permute-start(f32[16,8,768]{2,1,0:T(8,128)S(1)} %weighted_theirs.1), channel_id=1, source_target_pairs={{0,16},{16,0},{1,17},{17,1},{2,18},{18,2},{3,19},{19,3},{4,20},{20... | collective-permute-start | bytes 1179656 | tf_op jit(solution)/shard_map/ppermute | solution.py:267

commit v9 on v8

--- a/solution.py
+++ b/solution.py
@@ -47,41 +47,37 @@
                   log_s, cohort_s, seeds_s, sums_v, small_sems, sems):
     local_clients, row_count, width = held_ref.shape
     cohort_count = log_s.shape[0]
-    def arrival(c):
-        return pltpu.make_async_copy(updates_hbm.at[c], held_ref.at[c], sems.at[c])
-
-    early, ahead = 2, 6
-    for c in range(early):
-        arrival(c).start()
+    ends = [0, 4, 8, 11, 12]
+    copies = [
+        pltpu.make_async_copy(
+            updates_hbm.at[first:last], held_ref.at[first:last], sems.at[k]
+        ) for k, (first, last) in enumerate(zip(ends, ends[1:]))
+    ]
+    copies[0].start()
     small = []
     for k, (source, target) in enumerate((
         (log_hbm, log_s), (cohort_hbm, cohort_s), (seeds_hbm, seeds_s), (momentum_hbm, momentum_ref),
     )):
         small.append(pltpu.make_async_copy(source, target, small_sems.at[k]))
         small[-1].start()
-    for c in range(early, ahead):
-        arrival(c).start()
+    for copy in copies[1:]:
+        copy.start()
 
     step = 2 * PAIR
 
-    def add_client(c, follows):
-        arrival(c).wait()
-        if follows:
-            arrival(c + ahead).start()
+    def add_client(c, carry):
         acc = jnp.zeros((row_count, step), jnp.float32)
         for at in range(0, width, step):
             block = held_ref[c, :, at : at + step].astype(jnp.float32)
             acc = acc + block * block
         sums_v[c] = jnp.sum(fold(acc), axis=0, keepdims=True)
-
-    def add_clients(first, last, follows):
-        def step(c, carry):
-            add_client(c, follows)
-            return carry
-
-        lax.fori_loop(first, last, step, 0)
-
-    add_clients(0, early, True)
+        return carry
+
+    def add_clients(k):
+        copies[k].wait()
+        lax.fori_loop(ends[k], ends[k + 1], add_client, 0)
+
+    add_clients(0)
     for copy in small:
         copy.wait()
 
@@ -102,26 +98,16 @@
         member_ref[c : c + 1, :] = jnp.where((lanes & (HALF - 1)) == cohort, 1.0, 0.0)
     limit_ref[...] = jnp.exp(own_logs)
 
-    add_clients(early, local_clients - ahead, True)
-    add_clients(local_clients - ahead, local_clients, False)
+    for k in range(1, len(copies)):
+        add_clients(k)
     column = jnp.sum(sums_v[...][:, 0, :], axis=1, keepdims=True)
     row = jnp.sum(jnp.where(diagonal(local_clients), column, 0.0), axis=0, keepdims=True)
     partial_ref[...] = jnp.broadcast_to(row[None], partial_ref.shape)
 
 
-def weight_kernel(other, limit_ref, member_ref, squares_ref, held_ref, slab_ref):
+def write_slabs(odd, factors, counts, held_ref, slab_ref):
     local_clients, row_count, width = held_ref.shape
-    odd = (lax.axis_index("core") + other) % 2
-    norms = jnp.sqrt(jnp.sum(squares_ref[...], axis=0))
-    limit = limit_ref[...]
-    factor = limit / jnp.maximum(norms, limit)
-    factors = [jnp.broadcast_to(factor[:, c : c + 1], (row_count, REACH)) for c in range(local_clients)]
-    bit = (norms <= limit).astype(jnp.float32)
-    bits = jnp.sum(jnp.where(diagonal(local_clients), bit, 0.0), axis=1, keepdims=True)
-    counts = jnp.sum(member_ref[...] * bits, axis=0, keepdims=True)
-    eight = (8, LANES)
-    counts = jnp.where(row_ids(eight) == 0, counts, 0.0)
-    left = lane_ids(eight) < HALF
+    left = lane_ids((8, LANES)) < HALF
     spare_first = left & (odd == 1)
     spare_last = jnp.logical_not(left) & (odd == 0)
 
@@ -145,7 +131,35 @@
     lax.fori_loop(0, width // PAIR, pair, 0, unroll=4)
 
 
-def base_kernel(width, total_clients, band, round_s, coef_s, seeds_ref, log_ref, momentum_ref, base_ref):
+def theirs_kernel(limit_ref, member_ref, squares_ref, held_ref, slab_ref, factors_ref, counts_ref):
+    local_clients, row_count, _ = held_ref.shape
+    norms = jnp.sqrt(jnp.sum(squares_ref[...], axis=0))
+    limit = limit_ref[...]
+    factor = limit / jnp.maximum(norms, limit)
+    factors = [jnp.broadcast_to(factor[:, c : c + 1], (row_count, REACH)) for c in range(local_clients)]
+    for c in range(local_clients):
+        factors_ref[c : c + 1, :] = factors[c][:1, :LANES]
+    bit = (norms <= limit).astype(jnp.float32)
+    bits = jnp.sum(jnp.where(diagonal(local_clients), bit, 0.0), axis=1, keepdims=True)
+    counts = jnp.sum(member_ref[...] * bits, axis=0, keepdims=True)
+    counts = jnp.where(row_ids((8, LANES)) == 0, counts, 0.0)
+    counts_ref[...] = counts
+    write_slabs(1 - lax.axis_index("core"), factors, counts, held_ref, slab_ref)
+
+
+def own_kernel(width, total_clients, band, round_s, coef_s, seeds_ref, log_ref, momentum_ref,
+               factors_ref, counts_ref, held_ref, slab_ref, base_ref):
+    write_base(width, total_clients, band, round_s, coef_s, seeds_ref, log_ref, momentum_ref, base_ref)
+    local_clients, row_count, _ = held_ref.shape
+    factors = [
+        jnp.concatenate(
+            [jnp.broadcast_to(factors_ref[c : c + 1, :], (row_count, LANES))] * (REACH // LANES), axis=1
+        ) for c in range(local_clients)
+    ]
+    write_slabs(lax.axis_index("core"), factors, counts_ref[...], held_ref, slab_ref)
+
+
+def write_base(width, total_clients, band, round_s, coef_s, seeds_ref, log_ref, momentum_ref, base_ref):
     rows, cols = momentum_ref.shape
     first_row = lax.axis_index("shard") * rows
     first_col = (2 * lax.axis_index("chip") + lax.axis_index("core")) * cols
@@ -218,7 +232,7 @@
             pltpu.SMEM(seeds.shape, jnp.int32),
             pltpu.VMEM((local_clients, 1, LANES), jnp.float32),
             pltpu.SemaphoreType.DMA((4,)),
-            pltpu.SemaphoreType.DMA((local_clients,)),
+            pltpu.SemaphoreType.DMA((4,)),
         ],
         compiler_params=params,
         name="squares",
@@ -232,40 +246,35 @@
         partial, "shard", 0, 0, tiled=True, axis_index_groups=[list(range(shards))]
     )
 
-    def base_of(*refs):
-        base_kernel(width, total_clients, seeds.shape[0], *refs)
-
-    base = pl.pallas_call(
-        base_of,
-        out_shape=jax.ShapeDtypeStruct((rows, cols), jnp.float32),
-        in_specs=[smem] * 2 + [vmem] * 3,
-        out_specs=vmem,
+    slabs = jax.ShapeDtypeStruct((chips, 8, SLAB), jnp.float32)
+    theirs, factors, counts = pl.pallas_call(
+        theirs_kernel,
+        out_shape=(
+            slabs,
+            jax.ShapeDtypeStruct((local_clients, LANES), jnp.float32),
+            jax.ShapeDtypeStruct((8, LANES), jnp.float32),
+        ),
+        in_specs=[vmem] * 4,
+        out_specs=(vmem,) * 3,
+        compiler_params=params,
+        name="weighted_theirs",
+    )(limit, member, squares, held)
+    arrived = lax.ppermute(theirs, "core", [(0, 1), (1, 0)])
+
+    def own_of(*refs):
+        own_kernel(width, total_clients, seeds.shape[0], *refs)
+
+    own, base = pl.pallas_call(
+        own_of,
+        out_shape=(slabs, jax.ShapeDtypeStruct((rows, cols), jnp.float32)),
+        in_specs=[smem] * 2 + [vmem] * 6,
+        out_specs=(vmem,) * 2,
         compiler_params=params,
         cost_estimate=pl.CostEstimate(
-            flops=200 * momentum.size, bytes_accessed=8 * momentum.size, transcendentals=0
+            flops=2 * updates.size, bytes_accessed=updates.size, transcendentals=0
         ),
-        name="base",
-    )(round_index, coef_index, seed_row, log_row, momentum_v)
-
-    def weighted(other):
-        def weight(*refs):
-            weight_kernel(other, *refs)
-
-        return pl.pallas_call(
-            weight,
-            out_shape=jax.ShapeDtypeStruct((chips, 8, SLAB), jnp.float32),
-            in_specs=[vmem] * 4,
-            out_specs=vmem,
-            compiler_params=params,
-            cost_estimate=pl.CostEstimate(
-                flops=2 * updates.size, bytes_accessed=updates.size, transcendentals=0
-            ),
-            name="weighted_theirs" if other else "weighted_own",
-        )(limit, member, squares, held)
-
-    theirs = weighted(1)
-    arrived = lax.ppermute(theirs, "core", [(0, 1), (1, 0)])
-    own = weighted(0)
+        name="weighted_own",
+    )(round_index, coef_index, seed_row, log_row, momentum_v, factors, counts, held)
 
     both = pl.pallas_call(
         add_kernel,
@@ -275,7 +284,6 @@
         compiler_params=params,
         name="add_cores",
     )(own, arrived)
-    both, base = lax.optimization_barrier((both, base))
     parts = lax.all_to_all(both, "chip", 0, 0, tiled=True)
 
     def finish(*refs):

time: 54.7 us -> 54.3 us (level)
    pallas_call x3 -> x2, Pallas kernels: 1.76 us -> 1.66 us  [the longest x1 0.88 us: per_device(): pl.pallas_call(own_of, out_shape=(slabs, jax.ShapeDtypeStruct((rows, cols...]
where the time goes in v9:
time: 54.3 us; the launch traced here: 54.1 us
  blocking collectives  42.5 us (78%)
  Pallas kernels  5.65 us (10%)
  starting transfers between devices  4 us (7%)
  between operations  1.97 us (4%)
    all_to_all x1, blocking collectives, per_device(): lax.all_to_all(partial, 'shard', 0, 0, tiled=True, axis_index_groups=[lis...  26.8 us
    all_to_all x1, blocking collectives, per_device(): parts = lax.all_to_all(both, 'chip', 0, 0, tiled=True)  15.6 us
    ppermute x1, starting transfers between devices, per_device(): arrived = lax.ppermute(theirs, 'core', [(0, 1), (1, 0)])  4 us
    pallas_call x1, Pallas kernels, per_device(): pl.pallas_call(square_kernel, out_shape=(pltpu.VMEM(updates.shape, jnp.bf...  3.16 us
  transfers between devices with their start and end apart: 1, of which 0 were waited for; matrix products, arithmetic and copies ran while one was open for 0% of the time, Pallas kernels for 2%

profile of v9, /device:TPU:1, one launch (start us, length us, event | category | flops | bytes accessed | tf_op | source)
XLA Modules:
  0.0 54.1 jit_solution(13574030706699242059)
XLA Ops:
  0.6 3.2 %squares.1 = (bf16[12,12,14336]{2,1,0:T(8,128)(2,1)S(1)}, f32[16,1,128]{2,1,0:T(1,128)S(1)}, f32[12,448]{1,0:T(8,128)S(1)}, s32[1,128]{1,0:T(1,128)S(1)}, f32[1,...) custom-call(f32[12]{0:T(128)} %log_hbm.1, s32[384]{0:T(512)} %cohort_hbm.1, s32[8]{0:T(128)} %seeds_hbm.1, ...), custom_call_target="tpu_custom_call" | custom-call | tf_op jit(solution)/shard_map/squares/pallas_call | solution.py:216
  3.8 26.8 %all_to_all.10.squares_ref = f32[16,1,128]{2,1,0:T(1,128)S(1)} all-to-all(f32[16,1,128]{2,1,0:T(1,128)S(1)} %get-tuple-element.27), channel_id=1, replica_groups={{0,1,2,3,4,5,6,7,8,9,10,11,12,13,14,15},{16,17,18,19,20,21,22,23,24,25,..., dimensions={0} | all-to-all | bytes 16384 | tf_op jit(solution)/shard_map/all_to_all | solution.py:245
  30.6 0.8 %weighted_theirs.1 = (f32[16,8,768]{2,1,0:T(8,128)S(1)}, f32[12,128]{1,0:T(8,128)S(1)}, f32[8,128]{1,0:T(8,128)S(1)}) custom-call(f32[1,128]{1,0:T(1,128)S(1)} %get-tuple-element.25.limit_ref, f32[12,128]{1,0:T(8,128)S(1)} %get-tuple-element.26.member_ref, f32[16,1,128]{2,1,0:T(1,128)S(1)} %all_to_all.10.squares_ref, ...), custom_call_target="tpu_custom_call" | custom-call | tf_op jit(solution)/shard_map/weighted_theirs/pallas_call | solution.py:250
  31.4 4.0 %collective-permute-start = (f32[16,8,768]{2,1,0:T(8,128)S(1)}, f32[16,8,768]{2,1,0:T(8,128)S(1)}, u32[]{:S(2)}, u32[]{:S(2)}) collective-permute-start(f32[16,8,768]{2,1,0:T(8,128)S(1)} %get-tuple-element.33), channel_id=1, source_target_pairs={{0,16},{16,0},{1,17},{17,1},{2,18},{18,2},{3,19},{19,3},{4,20},{20... | collective-permute-start | bytes 1179656 | tf_op jit(solution)/shard_map/ppermute | solution.py:262
  36.7 0.9 %weighted_own.1 = (f32[16,8,768]{2,1,0:T(8,128)S(1)}, f32[12,448]{1,0:T(8,128)S(1)}) custom-call(s32[1]{0:T(128)S(6)} %copy.9.refs_0_, s32[1]{0:T(128)S(6)} %copy.10.refs_1_, s32[1,128]{1,0:T(1,128)S(1)} %get-tuple-element.23.refs_2_, f32[1,128]{1,0:T(1,128)S(1)} %get-tuple-element.19.refs_3_.refs_0_, f32[12,448]{1,0:T(8,128)S(1)} %get-tuple-element.24.refs_4_, ...), custom_call_target="tpu_custom_call" | custom-call | flops 4128768 | bytes 2064384 | tf_op jit(solution)/shard_map/weighted_own/pallas_call | solution.py:267
  37.6 0.0 collective-permute-done.other_ref
  37.7 15.6 %all_to_all.11.refs_2_ = f32[16,8,768]{2,1,0:T(8,128)S(1)} all-to-all(f32[16,8,768]{2,1,0:T(8,128)S(1)} %add_cores.1), channel_id=1, replica_groups=mesh['chip'=16,'core'=2,'shard'=16] {'chip'}, dimensions={0} | all-to-all | bytes 786432 | tf_op jit(solution)/shard_map/all_to_all | solution.py:287
  53.3 0.8 %finish.1 = (f32[12,448]{1,0:T(8,128)}, f32[1,12]{1,0:T(1,128)}) custom-call(f32[1,128]{1,0:T(1,128)S(1)} %get-tuple-element.19.refs_3_.refs_0_, f32[12,448]{1,0:T(8,128)S(1)} %get-tuple-element.31.refs_1_, f32[16,8,768]{2,1,0:T(8,128)S(1)} %all_to_all.11.refs_2_), custom_call_target="tpu_custom_call" | custom-call | tf_op jit(solution)/shard_map/finish/pallas_call | solution.py:292
  (1 shorter events, 0.0 us)
Async XLA Ops:
  31.4 6.2 %collective-permute-start = (f32[16,8,768]{2,1,0:T(8,128)S(1)}, f32[16,8,768]{2,1,0:T(8,128)S(1)}, u32[]{:S(2)}, u32[]{:S(2)}) collective-permute-start(f32[16,8,768]{2,1,0:T(8,128)S(1)} %get-tuple-element.33), channel_id=1, source_target_pairs={{0,16},{16,0},{1,17},{17,1},{2,18},{18,2},{3,19},{19,3},{4,20},{20... | collective-permute-start | bytes 1179656 | tf_op jit(solution)/shard_map/ppermute | solution.py:262

commit v10 on v9

--- a/solution.py
+++ b/solution.py
@@ -47,7 +47,7 @@
                   log_s, cohort_s, seeds_s, sums_v, small_sems, sems):
     local_clients, row_count, width = held_ref.shape
     cohort_count = log_s.shape[0]
-    ends = [0, 4, 8, 11, 12]
+    ends = [0, 6, 11, 12]
     copies = [
         pltpu.make_async_copy(
             updates_hbm.at[first:last], held_ref.at[first:last], sems.at[k]
@@ -189,13 +189,17 @@
 def finish_kernel(total_clients, cohort_count, log_ref, base_ref, slab_ref, momentum_ref, next_ref):
     cols = base_ref.shape[1]
     odd = lax.axis_index("core") == 1
-    total = jnp.sum(slab_ref[...], axis=0)
+    parts = [slab_ref[k] for k in range(slab_ref.shape[0])]
+    while len(parts) > 1:
+        parts = [sum(parts[at : at + 2]) for at in range(0, len(parts), 2)]
+    total = parts[0]
+    share = 1.0 / total_clients
     upper = total[:, :REACH]
     lower = jnp.concatenate([total[:4, REACH:], total[4:, REACH:]], axis=1)
     upper_own = jnp.where(odd, upper[:, HALF:], upper[:, :cols])
     lower_own = jnp.where(odd, lower[:, HALF:], lower[:, :cols])
-    momentum_ref[:8, :] = base_ref[:8, :] + upper_own / total_clients
-    momentum_ref[8:, :] = base_ref[8:, :] + lower_own / total_clients
+    momentum_ref[:8, :] = base_ref[:8, :] + upper_own * share
+    momentum_ref[8:, :] = base_ref[8:, :] + lower_own * share
     counts = jnp.where(odd, upper[:1, :cohort_count], upper[:1, cols : cols + cohort_count])
     next_ref[...] = log_ref[:, :cohort_count] - 0.2 * (counts / (total_clients // cohort_count) - 0.5)
 
@@ -232,7 +236,7 @@
             pltpu.SMEM(seeds.shape, jnp.int32),
             pltpu.VMEM((local_clients, 1, LANES), jnp.float32),
             pltpu.SemaphoreType.DMA((4,)),
-            pltpu.SemaphoreType.DMA((4,)),
+            pltpu.SemaphoreType.DMA((3,)),
         ],
         compiler_params=params,
         name="squares",

time: 54.3 us -> 54.3 us (level)
  no operation moved by 1% of the time
where the time goes in v10:
time: 54.3 us; the launch traced here: 54.1 us
  blocking collectives  42.5 us (78%)
  Pallas kernels  5.63 us (10%)
  starting transfers between devices  4 us (7%)
  between operations  1.97 us (4%)
    all_to_all x1, blocking collectives, per_device(): lax.all_to_all(partial, 'shard', 0, 0, tiled=True, axis_index_groups=[lis...  26.8 us
    all_to_all x1, blocking collectives, per_device(): parts = lax.all_to_all(both, 'chip', 0, 0, tiled=True)  15.6 us
    ppermute x1, starting transfers between devices, per_device(): arrived = lax.ppermute(theirs, 'core', [(0, 1), (1, 0)])  4 us
    pallas_call x1, Pallas kernels, per_device(): pl.pallas_call(square_kernel, out_shape=(pltpu.VMEM(updates.shape, jnp.bf...  3.15 us
  transfers between devices with their start and end apart: 1, of which 0 were waited for; matrix products, arithmetic and copies ran while one was open for 0% of the time, Pallas kernels for 2%

profile of v10, /device:TPU:1, one launch (start us, length us, event | category | flops | bytes accessed | tf_op | source)
XLA Modules:
  0.0 54.1 jit_solution(2973010538374435396)
XLA Ops:
  0.6 3.2 %squares.1 = (bf16[12,12,14336]{2,1,0:T(8,128)(2,1)S(1)}, f32[16,1,128]{2,1,0:T(1,128)S(1)}, f32[12,448]{1,0:T(8,128)S(1)}, s32[1,128]{1,0:T(1,128)S(1)}, f32[1,...) custom-call(f32[12]{0:T(128)} %log_hbm.1, s32[384]{0:T(512)} %cohort_hbm.1, s32[8]{0:T(128)} %seeds_hbm.1, ...), custom_call_target="tpu_custom_call" | custom-call | tf_op jit(solution)/shard_map/squares/pallas_call | solution.py:220
  3.8 26.8 %all_to_all.10.squares_ref = f32[16,1,128]{2,1,0:T(1,128)S(1)} all-to-all(f32[16,1,128]{2,1,0:T(1,128)S(1)} %get-tuple-element.27), channel_id=1, replica_groups={{0,1,2,3,4,5,6,7,8,9,10,11,12,13,14,15},{16,17,18,19,20,21,22,23,24,25,..., dimensions={0} | all-to-all | bytes 16384 | tf_op jit(solution)/shard_map/all_to_all | solution.py:249
  30.6 0.8 %weighted_theirs.1 = (f32[16,8,768]{2,1,0:T(8,128)S(1)}, f32[12,128]{1,0:T(8,128)S(1)}, f32[8,128]{1,0:T(8,128)S(1)}) custom-call(f32[1,128]{1,0:T(1,128)S(1)} %get-tuple-element.25.limit_ref, f32[12,128]{1,0:T(8,128)S(1)} %get-tuple-element.26.member_ref, f32[16,1,128]{2,1,0:T(1,128)S(1)} %all_to_all.10.squares_ref, ...), custom_call_target="tpu_custom_call" | custom-call | tf_op jit(solution)/shard_map/weighted_theirs/pallas_call | solution.py:254
  31.4 4.0 %collective-permute-start = (f32[16,8,768]{2,1,0:T(8,128)S(1)}, f32[16,8,768]{2,1,0:T(8,128)S(1)}, u32[]{:S(2)}, u32[]{:S(2)}) collective-permute-start(f32[16,8,768]{2,1,0:T(8,128)S(1)} %get-tuple-element.33), channel_id=1, source_target_pairs={{0,16},{16,0},{1,17},{17,1},{2,18},{18,2},{3,19},{19,3},{4,20},{20... | collective-permute-start | bytes 1179656 | tf_op jit(solution)/shard_map/ppermute | solution.py:266
  36.7 0.9 %weighted_own.1 = (f32[16,8,768]{2,1,0:T(8,128)S(1)}, f32[12,448]{1,0:T(8,128)S(1)}) custom-call(s32[1]{0:T(128)S(6)} %copy.9.refs_0_, s32[1]{0:T(128)S(6)} %copy.10.refs_1_, s32[1,128]{1,0:T(1,128)S(1)} %get-tuple-element.23.refs_2_, f32[1,128]{1,0:T(1,128)S(1)} %get-tuple-element.19.refs_3_.refs_0_, f32[12,448]{1,0:T(8,128)S(1)} %get-tuple-element.24.refs_4_, ...), custom_call_target="tpu_custom_call" | custom-call | flops 4128768 | bytes 2064384 | tf_op jit(solution)/shard_map/weighted_own/pallas_call | solution.py:271
  37.6 0.0 collective-permute-done.other_ref
  37.7 15.6 %all_to_all.11.refs_2_ = f32[16,8,768]{2,1,0:T(8,128)S(1)} all-to-all(f32[16,8,768]{2,1,0:T(8,128)S(1)} %add_cores.1), channel_id=1, replica_groups=mesh['chip'=16,'core'=2,'shard'=16] {'chip'}, dimensions={0} | all-to-all | bytes 786432 | tf_op jit(solution)/shard_map/all_to_all | solution.py:291
  53.3 0.8 %finish.1 = (f32[12,448]{1,0:T(8,128)}, f32[1,12]{1,0:T(1,128)}) custom-call(f32[1,128]{1,0:T(1,128)S(1)} %get-tuple-element.19.refs_3_.refs_0_, f32[12,448]{1,0:T(8,128)S(1)} %get-tuple-element.31.refs_1_, f32[16,8,768]{2,1,0:T(8,128)S(1)} %all_to_all.11.refs_2_), custom_call_target="tpu_custom_call" | custom-call | tf_op jit(solution)/shard_map/finish/pallas_call | solution.py:296
  (1 shorter events, 0.0 us)
Async XLA Ops:
  31.4 6.2 %collective-permute-start = (f32[16,8,768]{2,1,0:T(8,128)S(1)}, f32[16,8,768]{2,1,0:T(8,128)S(1)}, u32[]{:S(2)}, u32[]{:S(2)}) collective-permute-start(f32[16,8,768]{2,1,0:T(8,128)S(1)} %get-tuple-element.33), channel_id=1, source_target_pairs={{0,16},{16,0},{1,17},{17,1},{2,18},{18,2},{3,19},{19,3},{4,20},{20... | collective-permute-start | bytes 1179656 | tf_op jit(solution)/shard_map/ppermute | solution.py:266

commit v11 on v10

--- a/solution.py
+++ b/solution.py
@@ -128,7 +128,7 @@
             )
         return carry
 
-    lax.fori_loop(0, width // PAIR, pair, 0, unroll=4)
+    lax.fori_loop(0, width // PAIR, pair, 0, unroll=8)
 
 
 def theirs_kernel(limit_ref, member_ref, squares_ref, held_ref, slab_ref, factors_ref, counts_ref):

time: 54.3 us -> 54.3 us (level)
  no operation moved by 1% of the time
where the time goes in v11:
time: 54.3 us; the launch traced here: 54.1 us
  blocking collectives  42.5 us (78%)
  Pallas kernels  5.59 us (10%)
  starting transfers between devices  4 us (7%)
  between operations  1.97 us (4%)
    all_to_all x1, blocking collectives, per_device(): lax.all_to_all(partial, 'shard', 0, 0, tiled=True, axis_index_groups=[lis...  26.8 us
    all_to_all x1, blocking collectives, per_device(): parts = lax.all_to_all(both, 'chip', 0, 0, tiled=True)  15.6 us
    ppermute x1, starting transfers between devices, per_device(): arrived = lax.ppermute(theirs, 'core', [(0, 1), (1, 0)])  4 us
    pallas_call x1, Pallas kernels, per_device(): pl.pallas_call(square_kernel, out_shape=(pltpu.VMEM(updates.shape, jnp.bf...  3.15 us
  transfers between devices with their start and end apart: 1, of which 0 were waited for; matrix products, arithmetic and copies ran while one was open for 0% of the time, Pallas kernels for 2%

profile of v11, /device:TPU:1, one launch (start us, length us, event | category | flops | bytes accessed | tf_op | source)
XLA Modules:
  0.0 54.1 jit_solution(7941844049052245731)
XLA Ops:
  0.6 3.2 %squares.1 = (bf16[12,12,14336]{2,1,0:T(8,128)(2,1)S(1)}, f32[16,1,128]{2,1,0:T(1,128)S(1)}, f32[12,448]{1,0:T(8,128)S(1)}, s32[1,128]{1,0:T(1,128)S(1)}, f32[1,...) custom-call(f32[12]{0:T(128)} %log_hbm.1, s32[384]{0:T(512)} %cohort_hbm.1, s32[8]{0:T(128)} %seeds_hbm.1, ...), custom_call_target="tpu_custom_call" | custom-call | tf_op jit(solution)/shard_map/squares/pallas_call | solution.py:220
  3.8 26.8 %all_to_all.10.squares_ref = f32[16,1,128]{2,1,0:T(1,128)S(1)} all-to-all(f32[16,1,128]{2,1,0:T(1,128)S(1)} %get-tuple-element.27), channel_id=1, replica_groups={{0,1,2,3,4,5,6,7,8,9,10,11,12,13,14,15},{16,17,18,19,20,21,22,23,24,25,..., dimensions={0} | all-to-all | bytes 16384 | tf_op jit(solution)/shard_map/all_to_all | solution.py:249
  30.6 0.8 %weighted_theirs.1 = (f32[16,8,768]{2,1,0:T(8,128)S(1)}, f32[12,128]{1,0:T(8,128)S(1)}, f32[8,128]{1,0:T(8,128)S(1)}) custom-call(f32[1,128]{1,0:T(1,128)S(1)} %get-tuple-element.25.limit_ref, f32[12,128]{1,0:T(8,128)S(1)} %get-tuple-element.26.member_ref, f32[16,1,128]{2,1,0:T(1,128)S(1)} %all_to_all.10.squares_ref, ...), custom_call_target="tpu_custom_call" | custom-call | tf_op jit(solution)/shard_map/weighted_theirs/pallas_call | solution.py:254
  31.4 4.0 %collective-permute-start = (f32[16,8,768]{2,1,0:T(8,128)S(1)}, f32[16,8,768]{2,1,0:T(8,128)S(1)}, u32[]{:S(2)}, u32[]{:S(2)}) collective-permute-start(f32[16,8,768]{2,1,0:T(8,128)S(1)} %get-tuple-element.33), channel_id=1, source_target_pairs={{0,16},{16,0},{1,17},{17,1},{2,18},{18,2},{3,19},{19,3},{4,20},{20... | collective-permute-start | bytes 1179656 | tf_op jit(solution)/shard_map/ppermute | solution.py:266
  36.7 0.9 %weighted_own.1 = (f32[16,8,768]{2,1,0:T(8,128)S(1)}, f32[12,448]{1,0:T(8,128)S(1)}) custom-call(s32[1]{0:T(128)S(6)} %copy.9.refs_0_, s32[1]{0:T(128)S(6)} %copy.10.refs_1_, s32[1,128]{1,0:T(1,128)S(1)} %get-tuple-element.23.refs_2_, f32[1,128]{1,0:T(1,128)S(1)} %get-tuple-element.19.refs_3_.refs_0_, f32[12,448]{1,0:T(8,128)S(1)} %get-tuple-element.24.refs_4_, ...), custom_call_target="tpu_custom_call" | custom-call | flops 4128768 | bytes 2064384 | tf_op jit(solution)/shard_map/weighted_own/pallas_call | solution.py:271
  37.6 0.0 collective-permute-done.other_ref
  37.6 15.6 %all_to_all.11.refs_2_ = f32[16,8,768]{2,1,0:T(8,128)S(1)} all-to-all(f32[16,8,768]{2,1,0:T(8,128)S(1)} %add_cores.1), channel_id=1, replica_groups=mesh['chip'=16,'core'=2,'shard'=16] {'chip'}, dimensions={0} | all-to-all | bytes 786432 | tf_op jit(solution)/shard_map/all_to_all | solution.py:291
  53.3 0.8 %finish.1 = (f32[12,448]{1,0:T(8,128)}, f32[1,12]{1,0:T(1,128)}) custom-call(f32[1,128]{1,0:T(1,128)S(1)} %get-tuple-element.19.refs_3_.refs_0_, f32[12,448]{1,0:T(8,128)S(1)} %get-tuple-element.31.refs_1_, f32[16,8,768]{2,1,0:T(8,128)S(1)} %all_to_all.11.refs_2_), custom_call_target="tpu_custom_call" | custom-call | tf_op jit(solution)/shard_map/finish/pallas_call | solution.py:296
  (1 shorter events, 0.0 us)
Async XLA Ops:
  31.4 6.2 %collective-permute-start = (f32[16,8,768]{2,1,0:T(8,128)S(1)}, f32[16,8,768]{2,1,0:T(8,128)S(1)}, u32[]{:S(2)}, u32[]{:S(2)}) collective-permute-start(f32[16,8,768]{2,1,0:T(8,128)S(1)} %get-tuple-element.33), channel_id=1, source_target_pairs={{0,16},{16,0},{1,17},{17,1},{2,18},{18,2},{3,19},{19,3},{4,20},{20... | collective-permute-start | bytes 1179656 | tf_op jit(solution)/shard_map/ppermute | solution.py:266
